TPU v7x, 32 devices: a whole 2x2x4 slice. The times are simulated.
32 devices in a mesh: ctx: 8 (over y, x, core), exp: 4 (over z).
Axes of the slice: x: 2, y: 2, z: 4, core: 2. Of those that a mesh axis runs over, the one named last changes fastest.
Arguments:
- queries: bfloat16 [4096, 4096], P('ctx', 'exp'), may hold values from -6 to 6
- keys: bfloat16 [4096, 256], P('ctx'), may hold values from -6 to 6
- values: bfloat16 [4096, 256], P('ctx'), may hold values from -5 to 5
- residual: bfloat16 [4096, 4096], P(('ctx', 'exp')), may hold values from -12 to 12
- out_weight: bfloat16 [4096, 4096], P('exp'), may hold values from -0.25 to 0.25
- norm_gain: float32 [4096], replicated, may hold values from 0.5 to 1.5
- routes: int32 [4096, 8], P(('ctx', 'exp')), may hold values from 0 to 127, as said below
- chosen: int32 [4], replicated, may hold values from 0 to 127, as said below
- block_order: int32 [16], replicated, may hold values from 0 to 15, each once
Outputs:
- stream: bfloat16 [4096, 4096], P(('ctx', 'exp'))
- grams: float32 [4, 4096, 4096], P('exp', 'ctx')
Inputs may be any that keep to these rules, and one draw needn't show every extreme that they name: `routes`: each row names 8 different experts. In each aligned block of 128 rows (the rows of one device) no expert is named more than 16 times, and in every block some chosen expert is named exactly 16 times. `chosen`: 4 different experts, among them expert 0 and expert 128 - 1.
All inputs are finite; a program needn't handle non-finite values.
Results may differ from a plain program's by a relative error of at most 0.0085.
Values may be sent and summed in bfloat16 or wider, within the bound.
No kernel may reach another device: no remote copies, remote signals or barrier semaphores. Data moves between devices by JAX's collectives and lax.ppermute only.
A program may use at most 128 MiB of HBM per device.

v0:
```python
import jax
import jax.numpy as jnp
from jax import lax
from jax.sharding import PartitionSpec as P

QH = 32
KVH = 2
HD = 128
NE = 128
TOP = 8


def from_behind(block, axis, distance):
    devices = range(lax.axis_size(axis))
    route = [((i - distance) % len(devices), i) for i in devices]
    return lax.ppermute(block, axis, route)


def gram_update(shard_rows, ctx_rank, rows_dev):
    own_cols = lax.dynamic_slice_in_dim(shard_rows, ctx_rank * rows_dev, rows_dev, 1)
    product = lax.dot_general(
        own_cols, shard_rows, (((0,), (0,)), ((), ())), preferred_element_type=jnp.float32
    )
    return product


def local(queries, keys, values, residual, out_weight, norm_gain, routes, chosen, block_order):
    ctx_count = lax.axis_size("ctx")
    ctx_rank = lax.axis_index("ctx")
    column = lax.axis_index("exp")
    local_len = queries.shape[0]
    block_len = local_len // 2
    heads_here = queries.shape[1] // HD
    kv_head = column * heads_here // (QH // KVH)
    key_mine = lax.dynamic_slice_in_dim(keys, kv_head * HD, HD, 1)
    value_mine = lax.dynamic_slice_in_dim(values, kv_head * HD, HD, 1)
    kv_pair = jnp.stack([key_mine, value_mine])
    query_heads = queries.reshape(local_len, heads_here, HD)
    score_scale = HD ** (-0.5)

    def places(owner_idx):
        firsts = lax.dynamic_slice_in_dim(block_order, 2 * owner_idx, 2, 0)
        offsets = jnp.arange(local_len, dtype=jnp.int32)
        block_start = jnp.where(offsets // block_len == 0, firsts[0], firsts[1])
        return block_start * block_len + offsets % block_len

    query_pos = places(ctx_rank)

    def absorb(softmax_state, pair_now, owner_idx):
        key_pos = places(owner_idx)
        visible = key_pos[None, :] <= query_pos[:, None]

        def update(carried):
            run_max, run_sum, run_acc = carried
            scores = (
                jnp.einsum(
                    "qhd,kd->hqk", query_heads, pair_now[0], preferred_element_type=jnp.float32
                )
                * score_scale
            )
            scores = jnp.where(visible[None], scores, -1e30)
            new_max = jnp.maximum(run_max, jnp.max(scores, axis=2))
            unnormed = jnp.where(visible[None], jnp.exp(scores - new_max[:, :, None]), 0.0)
            shrink = jnp.exp(run_max - new_max)
            new_sum = run_sum * shrink + jnp.sum(unnormed, axis=2)
            added = jnp.einsum(
                "hqk,kd->hqd",
                unnormed.astype(jnp.bfloat16),
                pair_now[1],
                preferred_element_type=jnp.float32,
            )
            return (new_max, new_sum, run_acc * shrink[:, :, None] + added)

        return lax.cond(jnp.any(visible), update, lambda carried: carried, softmax_state)

    softmax_state = (
        jnp.full((heads_here, local_len), -1e30, jnp.float32),
        jnp.zeros((heads_here, local_len), jnp.float32),
        jnp.zeros((heads_here, local_len, HD), jnp.float32),
    )
    softmax_state = absorb(softmax_state, kv_pair, ctx_rank)

    def cycle_turn(cycle_step, carried):
        pair_now, state_now = carried
        pair_now = from_behind(pair_now, "ctx", 1)
        return (pair_now, absorb(state_now, pair_now, (ctx_rank - cycle_step) % ctx_count))

    _, softmax_state = lax.fori_loop(1, ctx_count, cycle_turn, (kv_pair, softmax_state))
    attention = (softmax_state[2] / softmax_state[1][:, :, None]).astype(jnp.bfloat16)
    attention = attention.transpose(1, 0, 2).reshape(local_len, heads_here * HD)
    token_rows = residual.shape[0]
    projection = lax.psum_scatter(
        jnp.dot(attention, out_weight, preferred_element_type=jnp.float32).astype(jnp.bfloat16),
        "exp",
        scatter_dimension=0,
        tiled=True,
    ).astype(jnp.float32)
    stream = (residual.astype(jnp.float32) + projection).astype(jnp.bfloat16)
    widened = stream.astype(jnp.float32)
    normed = (
        widened * lax.rsqrt(jnp.mean(widened * widened, axis=1, keepdims=True) + 1e-06) * norm_gain
    ).astype(jnp.bfloat16)
    routed = jnp.any(routes[:, :, None] == chosen[None, None, :], axis=1)
    arrival = jnp.cumsum(routed.astype(jnp.int32), axis=0) - 1
    capacity = 2 * token_rows * TOP // NE
    slot_ids = jnp.arange(capacity, dtype=jnp.int32)
    placing = (routed.T[:, None, :] & (arrival.T[:, None, :] == slot_ids[None, :, None])).astype(
        jnp.bfloat16
    )
    outgoing = jnp.einsum(
        "est,td->esd", placing, normed, preferred_element_type=jnp.float32
    ).astype(jnp.bfloat16)
    features = normed.shape[1]
    rows_dev = features // ctx_count
    arrived = lax.all_to_all(outgoing, "exp", split_axis=0, concat_axis=0, tiled=True)
    running = gram_update(
        lax.all_gather(arrived, "ctx", axis=0, tiled=True).reshape(-1, features), ctx_rank, rows_dev
    )
    mean_rows = local_len * ctx_count * TOP // NE
    return (stream, (running / mean_rows)[None])


def solution(mesh):
    in_specs = (
        P("ctx", "exp"),
        P("ctx", None),
        P("ctx", None),
        P(("ctx", "exp"), None),
        P("exp", None),
        P(),
        P(("ctx", "exp"), None),
        P(),
        P(),
    )
    out_specs = (P(("ctx", "exp"), None), P("exp", "ctx", None))
    return jax.shard_map(local, mesh=mesh, in_specs=in_specs, out_specs=out_specs, check_vma=False)
```

profile of v0, /device:TPU:0, one launch (start us, length us, event | category | flops | bytes accessed | tf_op | source)
XLA Modules:
  0.0 311.3 jit_solution(13479574769711250441)
XLA Ops:
  10.7 1.5 copy.36
  15.2 9.6 %conditional.2 = (f32[8,512]{1,0:T(8,128)}, f32[8,512]{1,0:T(8,128)S(1)}, f32[8,512,128]{2,1,0:T(8,128)S(1)}) conditional(s32[]{:T(128)} %convert_element_type.49, () %tuple.48, (pred[512,512]{0,1:T(8,128)(4,1)S(1)}, bf16[512,128]{1,0:T(8,128)(2,1)S(1)}, bf16[512,8,128]{0,2,1:T(8,128)(2,1)S(1)}, bf16[512,128]{1,0:T(8,128)(2,1)S(1)}) %tuple.102), branch_computations={%region_1.2_spmd, %region_2.5_spmd} | conditional | flops 1101545472 | bytes 29540376 | solution.py:74
  15.2 1.5 fusion.2
  17.4 3.8 %fusion.8 = f32[8,512,128]{2,1,0:T(8,128)S(1)} fusion(f32[512,512,8]{1,0,2:T(8,128)S(1)} %get-tuple-element.420, f32[8,512]{1,0:T(8,128)} %get-tuple-element.517, pred[512,512]{0,1:T(8,128)(4,1)S(1)} %get-tuple-element.289, f32[8,512]{1,0:T(8,128)S(1)} %get-tuple-element.413, bf16[512,128]{1,0:T(8,128)(2,1)S(1)} %get-tuple-element.292), kind=kOutput, calls=%fused_computation.8 | convolution fusion | flops 547880960 | bytes 10911744 | tf_op jit(solution)/shard_map/cond/branch_1_fun/hqk,kd->hqd/dot_general | solution.py:66
  21.2 2.7 fusion.4
  24.9 1.3 copy-done
  26.2 124.4 %while.23 = (s32[]{:T(128)}, bf16[2,512,128]{2,1,0:T(8,128)(2,1)}, f32[8,512]{1,0:T(8,128)}, f32[8,512]{1,0:T(8,128)S(1)}, f32[8,512,128]{2,1,0:T(8,128)}, /*ind...) while((s32[]{:T(128)}, bf16[2,512,128]{2,1,0:T(8,128)(2,1)}, ...), condition=%wide.region_11.12_spmd.clone, body=%wide.region_5.11_spmd.clone.sunk | while | flops 1102602240 | bytes 50340412 | solution.py:88
  27.3 1.3 multiply_add_fusion.7
  28.6 1.2 multiply_add_fusion.6
  31.3 2.5 collective-permute-done
  33.8 10.1 %conditional.5 = ((f32[8,512]{1,0:T(8,128)}, f32[8,512]{1,0:T(8,128)S(1)}, f32[8,512,128]{2,1,0:T(8,128)})) conditional(s32[]{:T(128)} %convert_element_type.92, (f32[8,512]{1,0:T(8,128)}, f32[8,512]{1,0:T(8,128)S(1)}, f32[8,512,128]{2,1,0:T(8,128)}) %tuple.87, (pred[512,512]{0,1:T(8,128)(4,1)S(1)}, bf16[2,512,128]{2,1,0:T(8,128)(2,1)S(1)}, ...), branch_computations={%region_7.7_spmd, %region_8.10_spmd} | conditional | flops 1102061568 | bytes 48496728 | solution.py:74
  33.8 1.5 fusion.18
  36.0 2.0 fusion.20
  38.8 3.1 %multiply_add_fusion = f32[8,512,128]{2,1,0:T(8,128)S(1)} fusion(f32[8,512,128]{2,1,0:T(8,128)S(1)} %copy-done.1, f32[512,512,8]{1,0,2:T(8,128)S(1)} %get-tuple-element.422, f32[8,512]{1,0:T(8,128)S(1)} %max.2, pred[512,512]{0,1:T(8,128)(4,1)S(1)} %get-tuple-element.294, f32[8,512]{1,0:T(8,128)S(1)} %get-tuple-element.416, ...), kind=kOutput, calls=%fused_computation.25 | convolution fusion | flops 548405248 | bytes 13008896 | tf_op jit(solution)/shard_map/while/body/eval_jaxpr/cond/branch_1_fun/hqk,kd->hqd/dot_general | solution.py:66
  41.9 1.3 copy-done.2
  45.3 1.3 multiply_add_fusion.7
  49.3 2.2 collective-permute-done
  51.5 10.1 %conditional.5 = ((f32[8,512]{1,0:T(8,128)}, f32[8,512]{1,0:T(8,128)S(1)}, f32[8,512,128]{2,1,0:T(8,128)})) conditional(s32[]{:T(128)} %convert_element_type.92, (f32[8,512]{1,0:T(8,128)}, f32[8,512]{1,0:T(8,128)S(1)}, f32[8,512,128]{2,1,0:T(8,128)}) %tuple.87, (pred[512,512]{0,1:T(8,128)(4,1)S(1)}, bf16[2,512,128]{2,1,0:T(8,128)(2,1)S(1)}, ...), branch_computations={%region_7.7_spmd, %region_8.10_spmd} | conditional | flops 1102061568 | bytes 48496728 | solution.py:74
  51.5 1.5 fusion.18
  53.7 2.0 fusion.20
  56.5 3.1 %multiply_add_fusion = f32[8,512,128]{2,1,0:T(8,128)S(1)} fusion(f32[8,512,128]{2,1,0:T(8,128)S(1)} %copy-done.1, f32[512,512,8]{1,0,2:T(8,128)S(1)} %get-tuple-element.422, f32[8,512]{1,0:T(8,128)S(1)} %max.2, pred[512,512]{0,1:T(8,128)(4,1)S(1)} %get-tuple-element.294, f32[8,512]{1,0:T(8,128)S(1)} %get-tuple-element.416, ...), kind=kOutput, calls=%fused_computation.25 | convolution fusion | flops 548405248 | bytes 13008896 | tf_op jit(solution)/shard_map/while/body/eval_jaxpr/cond/branch_1_fun/hqk,kd->hqd/dot_general | solution.py:66
  59.6 1.3 copy-done.2
  62.9 1.3 multiply_add_fusion.7
  66.9 2.3 collective-permute-done
  69.1 10.1 %conditional.5 = ((f32[8,512]{1,0:T(8,128)}, f32[8,512]{1,0:T(8,128)S(1)}, f32[8,512,128]{2,1,0:T(8,128)})) conditional(s32[]{:T(128)} %convert_element_type.92, (f32[8,512]{1,0:T(8,128)}, f32[8,512]{1,0:T(8,128)S(1)}, f32[8,512,128]{2,1,0:T(8,128)}) %tuple.87, (pred[512,512]{0,1:T(8,128)(4,1)S(1)}, bf16[2,512,128]{2,1,0:T(8,128)(2,1)S(1)}, ...), branch_computations={%region_7.7_spmd, %region_8.10_spmd} | conditional | flops 1102061568 | bytes 48496728 | solution.py:74
  69.1 1.5 fusion.18
  71.4 2.0 fusion.20
  74.1 3.1 %multiply_add_fusion = f32[8,512,128]{2,1,0:T(8,128)S(1)} fusion(f32[8,512,128]{2,1,0:T(8,128)S(1)} %copy-done.1, f32[512,512,8]{1,0,2:T(8,128)S(1)} %get-tuple-element.422, f32[8,512]{1,0:T(8,128)S(1)} %max.2, pred[512,512]{0,1:T(8,128)(4,1)S(1)} %get-tuple-element.294, f32[8,512]{1,0:T(8,128)S(1)} %get-tuple-element.416, ...), kind=kOutput, calls=%fused_computation.25 | convolution fusion | flops 548405248 | bytes 13008896 | tf_op jit(solution)/shard_map/while/body/eval_jaxpr/cond/branch_1_fun/hqk,kd->hqd/dot_general | solution.py:66
  77.3 1.3 copy-done.2
  80.6 1.3 multiply_add_fusion.7
  84.5 2.3 collective-permute-done
  86.8 10.1 %conditional.5 = ((f32[8,512]{1,0:T(8,128)}, f32[8,512]{1,0:T(8,128)S(1)}, f32[8,512,128]{2,1,0:T(8,128)})) conditional(s32[]{:T(128)} %convert_element_type.92, (f32[8,512]{1,0:T(8,128)}, f32[8,512]{1,0:T(8,128)S(1)}, f32[8,512,128]{2,1,0:T(8,128)}) %tuple.87, (pred[512,512]{0,1:T(8,128)(4,1)S(1)}, bf16[2,512,128]{2,1,0:T(8,128)(2,1)S(1)}, ...), branch_computations={%region_7.7_spmd, %region_8.10_spmd} | conditional | flops 1102061568 | bytes 48496728 | solution.py:74
  86.8 1.5 fusion.18
  89.0 2.0 fusion.20
  91.8 3.1 %multiply_add_fusion = f32[8,512,128]{2,1,0:T(8,128)S(1)} fusion(f32[8,512,128]{2,1,0:T(8,128)S(1)} %copy-done.1, f32[512,512,8]{1,0,2:T(8,128)S(1)} %get-tuple-element.422, f32[8,512]{1,0:T(8,128)S(1)} %max.2, pred[512,512]{0,1:T(8,128)(4,1)S(1)} %get-tuple-element.294, f32[8,512]{1,0:T(8,128)S(1)} %get-tuple-element.416, ...), kind=kOutput, calls=%fused_computation.25 | convolution fusion | flops 548405248 | bytes 13008896 | tf_op jit(solution)/shard_map/while/body/eval_jaxpr/cond/branch_1_fun/hqk,kd->hqd/dot_general | solution.py:66
  95.0 1.3 copy-done.2
  98.2 1.3 multiply_add_fusion.7
  102.2 2.3 collective-permute-done
  104.5 10.1 %conditional.5 = ((f32[8,512]{1,0:T(8,128)}, f32[8,512]{1,0:T(8,128)S(1)}, f32[8,512,128]{2,1,0:T(8,128)})) conditional(s32[]{:T(128)} %convert_element_type.92, (f32[8,512]{1,0:T(8,128)}, f32[8,512]{1,0:T(8,128)S(1)}, f32[8,512,128]{2,1,0:T(8,128)}) %tuple.87, (pred[512,512]{0,1:T(8,128)(4,1)S(1)}, bf16[2,512,128]{2,1,0:T(8,128)(2,1)S(1)}, ...), branch_computations={%region_7.7_spmd, %region_8.10_spmd} | conditional | flops 1102061568 | bytes 48496728 | solution.py:74
  104.5 1.5 fusion.18
  106.7 2.0 fusion.20
  109.5 3.1 %multiply_add_fusion = f32[8,512,128]{2,1,0:T(8,128)S(1)} fusion(f32[8,512,128]{2,1,0:T(8,128)S(1)} %copy-done.1, f32[512,512,8]{1,0,2:T(8,128)S(1)} %get-tuple-element.422, f32[8,512]{1,0:T(8,128)S(1)} %max.2, pred[512,512]{0,1:T(8,128)(4,1)S(1)} %get-tuple-element.294, f32[8,512]{1,0:T(8,128)S(1)} %get-tuple-element.416, ...), kind=kOutput, calls=%fused_computation.25 | convolution fusion | flops 548405248 | bytes 13008896 | tf_op jit(solution)/shard_map/while/body/eval_jaxpr/cond/branch_1_fun/hqk,kd->hqd/dot_general | solution.py:66
  112.6 1.3 copy-done.2
  115.9 1.3 multiply_add_fusion.7
  119.9 2.3 collective-permute-done
  122.1 10.1 %conditional.5 = ((f32[8,512]{1,0:T(8,128)}, f32[8,512]{1,0:T(8,128)S(1)}, f32[8,512,128]{2,1,0:T(8,128)})) conditional(s32[]{:T(128)} %convert_element_type.92, (f32[8,512]{1,0:T(8,128)}, f32[8,512]{1,0:T(8,128)S(1)}, f32[8,512,128]{2,1,0:T(8,128)}) %tuple.87, (pred[512,512]{0,1:T(8,128)(4,1)S(1)}, bf16[2,512,128]{2,1,0:T(8,128)(2,1)S(1)}, ...), branch_computations={%region_7.7_spmd, %region_8.10_spmd} | conditional | flops 1102061568 | bytes 48496728 | solution.py:74
  122.1 1.5 fusion.18
  124.4 2.0 fusion.20
  127.1 3.1 %multiply_add_fusion = f32[8,512,128]{2,1,0:T(8,128)S(1)} fusion(f32[8,512,128]{2,1,0:T(8,128)S(1)} %copy-done.1, f32[512,512,8]{1,0,2:T(8,128)S(1)} %get-tuple-element.422, f32[8,512]{1,0:T(8,128)S(1)} %max.2, pred[512,512]{0,1:T(8,128)(4,1)S(1)} %get-tuple-element.294, f32[8,512]{1,0:T(8,128)S(1)} %get-tuple-element.416, ...), kind=kOutput, calls=%fused_computation.25 | convolution fusion | flops 548405248 | bytes 13008896 | tf_op jit(solution)/shard_map/while/body/eval_jaxpr/cond/branch_1_fun/hqk,kd->hqd/dot_general | solution.py:66
  130.3 1.3 copy-done.2
  133.6 1.3 multiply_add_fusion.7
  137.5 2.3 collective-permute-done
  139.8 10.1 %conditional.5 = ((f32[8,512]{1,0:T(8,128)}, f32[8,512]{1,0:T(8,128)S(1)}, f32[8,512,128]{2,1,0:T(8,128)})) conditional(s32[]{:T(128)} %convert_element_type.92, (f32[8,512]{1,0:T(8,128)}, f32[8,512]{1,0:T(8,128)S(1)}, f32[8,512,128]{2,1,0:T(8,128)}) %tuple.87, (pred[512,512]{0,1:T(8,128)(4,1)S(1)}, bf16[2,512,128]{2,1,0:T(8,128)(2,1)S(1)}, ...), branch_computations={%region_7.7_spmd, %region_8.10_spmd} | conditional | flops 1102061568 | bytes 48496728 | solution.py:74
  139.8 1.5 fusion.18
  142.1 2.0 fusion.20
  144.8 3.1 %multiply_add_fusion = f32[8,512,128]{2,1,0:T(8,128)S(1)} fusion(f32[8,512,128]{2,1,0:T(8,128)S(1)} %copy-done.1, f32[512,512,8]{1,0,2:T(8,128)S(1)} %get-tuple-element.422, f32[8,512]{1,0:T(8,128)S(1)} %max.2, pred[512,512]{0,1:T(8,128)(4,1)S(1)} %get-tuple-element.294, f32[8,512]{1,0:T(8,128)S(1)} %get-tuple-element.416, ...), kind=kOutput, calls=%fused_computation.25 | convolution fusion | flops 548405248 | bytes 13008896 | tf_op jit(solution)/shard_map/while/body/eval_jaxpr/cond/branch_1_fun/hqk,kd->hqd/dot_general | solution.py:66
  148.0 1.3 copy-done.2
  150.6 1.9 copy.39
  152.9 9.6 %convolution_convert_fusion = bf16[512,4096]{1,0:T(8,128)(2,1)} fusion(bf16[512,1024]{0,1:T(8,128)(2,1)S(1)} %bitcast.76, bf16[1024,4096]{1,0:T(8,128)(2,1)} %param.19), kind=kOutput, calls=%fused_computation.53 | convolution fusion | flops 4297064448 | bytes 13631488 | tf_op jit(solution)/shard_map/dot_general | solution.py:93
  163.0 76.5 %reduce-scatter.2.cloned.1.call-done = bf16[128,4096]{1,0:T(8,128)(2,1)} async-done(((bf16[512,4096]{1,0:T(8,128)(2,1)}), bf16[128,4096]{1,0:T(8,128)(2,1)}) %reduce-scatter.2.cloned.1.call-update) | async-done | bytes 1048592 | tf_op jit(solution)/shard_map/reduce_scatter | solution.py:92
  239.5 1.7 fusion.43
  241.8 18.6 %all_to_all.5 = bf16[4,16,4096]{2,1,0:T(8,128)(2,1)} all-to-all(bf16[4,16,4096]{2,1,0:T(8,128)(2,1)S(1)} %convolution_convert_fusion.1), channel_id=1, replica_groups=mesh['ctx'=8,'exp'=4] {'exp'}, dimensions={0} | all-to-all | bytes 1048576 | tf_op jit(solution)/shard_map/all_to_all | solution.py:115
  260.4 35.9 %all-gather.2.cloned.1.call-done = bf16[32,16,4096]{2,1,0:T(8,128)(2,1)} async-done(((bf16[4,16,4096]{2,1,0:T(8,128)(2,1)}), bf16[32,16,4096]{2,1,0:T(8,128)(2,1)}) %all-gather.2.cloned.1.call-update) | async-done | bytes 4194320 | tf_op jit(solution)/shard_map/all_gather | solution.py:117
  296.4 8.1 %multiply_bitcast_fusion = f32[1,512,4096]{2,1,0:T(8,128)} fusion(bf16[512,4096]{1,0:T(8,128)(2,1)} %bitcast.74, s32[]{:T(128)S(6)} %select_n.161), kind=kOutput, calls=%fused_computation.52 | convolution fusion | flops 2149580800 | bytes 13107204 | tf_op jit(solution)/shard_map/dot_general | solution.py:21
  (118 shorter events, 46.9 us)
Async XLA Ops:
  7.2 232.4 %reduce-scatter.2.cloned.1.call-start = ((), (), s32[]{:S(2)}) async-start(), calls=%async_computation.2 | async-start | bytes 5242880 | tf_op jit(solution)/shard_map/reduce_scatter | solution.py:92
  15.2 11.0 %copy-start.8 = (s32[16]{0:T(128)S(1)}, s32[16]{0:T(128)}, u32[]{:S(2)}) copy-start(s32[16]{0:T(128)} %param.23) | copy-start | bytes 196
  24.9 1.3 copy-start
  26.2 7.6 %collective-permute-start = (bf16[2,512,128]{2,1,0:T(8,128)(2,1)}, bf16[2,512,128]{2,1,0:T(8,128)(2,1)S(1)}, u32[]{:S(2)}, u32[]{:S(2)}) collective-permute-start(bf16[2,512,128]{2,1,0:T(8,128)(2,1)} %get-tuple-element.537), channel_id=1, source_target_pairs={{28,0},{0,4},{4,8},{8,12},{12,16},{16,20},{20,24},{24,28},{29,1},{... | collective-permute-start | bytes 786440 | tf_op jit(solution)/shard_map/while/body/eval_jaxpr/ppermute | solution.py:16
  33.8 5.0 %copy-start.1 = (f32[8,512,128]{2,1,0:T(8,128)S(1)}, f32[8,512,128]{2,1,0:T(8,128)}, u32[]{:S(2)}) copy-start(f32[8,512,128]{2,1,0:T(8,128)} %get-tuple-element.298) | copy-start | bytes 6291460 | tf_op jit(solution)/shard_map/while/body/eval_jaxpr/cond
  41.9 1.3 copy-start.2
  44.6 6.9 %collective-permute-start = (bf16[2,512,128]{2,1,0:T(8,128)(2,1)}, bf16[2,512,128]{2,1,0:T(8,128)(2,1)S(1)}, u32[]{:S(2)}, u32[]{:S(2)}) collective-permute-start(bf16[2,512,128]{2,1,0:T(8,128)(2,1)} %get-tuple-element.537), channel_id=1, source_target_pairs={{28,0},{0,4},{4,8},{8,12},{12,16},{16,20},{20,24},{24,28},{29,1},{... | collective-permute-start | bytes 786440 | tf_op jit(solution)/shard_map/while/body/eval_jaxpr/ppermute | solution.py:16
  51.5 5.0 %copy-start.1 = (f32[8,512,128]{2,1,0:T(8,128)S(1)}, f32[8,512,128]{2,1,0:T(8,128)}, u32[]{:S(2)}) copy-start(f32[8,512,128]{2,1,0:T(8,128)} %get-tuple-element.298) | copy-start | bytes 6291460 | tf_op jit(solution)/shard_map/while/body/eval_jaxpr/cond
  59.6 1.3 copy-start.2
  62.2 6.9 %collective-permute-start = (bf16[2,512,128]{2,1,0:T(8,128)(2,1)}, bf16[2,512,128]{2,1,0:T(8,128)(2,1)S(1)}, u32[]{:S(2)}, u32[]{:S(2)}) collective-permute-start(bf16[2,512,128]{2,1,0:T(8,128)(2,1)} %get-tuple-element.537), channel_id=1, source_target_pairs={{28,0},{0,4},{4,8},{8,12},{12,16},{16,20},{20,24},{24,28},{29,1},{... | collective-permute-start | bytes 786440 | tf_op jit(solution)/shard_map/while/body/eval_jaxpr/ppermute | solution.py:16
  69.1 5.0 %copy-start.1 = (f32[8,512,128]{2,1,0:T(8,128)S(1)}, f32[8,512,128]{2,1,0:T(8,128)}, u32[]{:S(2)}) copy-start(f32[8,512,128]{2,1,0:T(8,128)} %get-tuple-element.298) | copy-start | bytes 6291460 | tf_op jit(solution)/shard_map/while/body/eval_jaxpr/cond
  77.3 1.3 copy-start.2
  79.9 6.9 %collective-permute-start = (bf16[2,512,128]{2,1,0:T(8,128)(2,1)}, bf16[2,512,128]{2,1,0:T(8,128)(2,1)S(1)}, u32[]{:S(2)}, u32[]{:S(2)}) collective-permute-start(bf16[2,512,128]{2,1,0:T(8,128)(2,1)} %get-tuple-element.537), channel_id=1, source_target_pairs={{28,0},{0,4},{4,8},{8,12},{12,16},{16,20},{20,24},{24,28},{29,1},{... | collective-permute-start | bytes 786440 | tf_op jit(solution)/shard_map/while/body/eval_jaxpr/ppermute | solution.py:16
  86.8 5.0 %copy-start.1 = (f32[8,512,128]{2,1,0:T(8,128)S(1)}, f32[8,512,128]{2,1,0:T(8,128)}, u32[]{:S(2)}) copy-start(f32[8,512,128]{2,1,0:T(8,128)} %get-tuple-element.298) | copy-start | bytes 6291460 | tf_op jit(solution)/shard_map/while/body/eval_jaxpr/cond
  94.9 1.3 copy-start.2
  97.6 6.9 %collective-permute-start = (bf16[2,512,128]{2,1,0:T(8,128)(2,1)}, bf16[2,512,128]{2,1,0:T(8,128)(2,1)S(1)}, u32[]{:S(2)}, u32[]{:S(2)}) collective-permute-start(bf16[2,512,128]{2,1,0:T(8,128)(2,1)} %get-tuple-element.537), channel_id=1, source_target_pairs={{28,0},{0,4},{4,8},{8,12},{12,16},{16,20},{20,24},{24,28},{29,1},{... | collective-permute-start | bytes 786440 | tf_op jit(solution)/shard_map/while/body/eval_jaxpr/ppermute | solution.py:16
  104.5 5.0 %copy-start.1 = (f32[8,512,128]{2,1,0:T(8,128)S(1)}, f32[8,512,128]{2,1,0:T(8,128)}, u32[]{:S(2)}) copy-start(f32[8,512,128]{2,1,0:T(8,128)} %get-tuple-element.298) | copy-start | bytes 6291460 | tf_op jit(solution)/shard_map/while/body/eval_jaxpr/cond
  112.6 1.3 copy-start.2
  115.2 6.9 %collective-permute-start = (bf16[2,512,128]{2,1,0:T(8,128)(2,1)}, bf16[2,512,128]{2,1,0:T(8,128)(2,1)S(1)}, u32[]{:S(2)}, u32[]{:S(2)}) collective-permute-start(bf16[2,512,128]{2,1,0:T(8,128)(2,1)} %get-tuple-element.537), channel_id=1, source_target_pairs={{28,0},{0,4},{4,8},{8,12},{12,16},{16,20},{20,24},{24,28},{29,1},{... | collective-permute-start | bytes 786440 | tf_op jit(solution)/shard_map/while/body/eval_jaxpr/ppermute | solution.py:16
  122.1 5.0 %copy-start.1 = (f32[8,512,128]{2,1,0:T(8,128)S(1)}, f32[8,512,128]{2,1,0:T(8,128)}, u32[]{:S(2)}) copy-start(f32[8,512,128]{2,1,0:T(8,128)} %get-tuple-element.298) | copy-start | bytes 6291460 | tf_op jit(solution)/shard_map/while/body/eval_jaxpr/cond
  130.3 1.3 copy-start.2
  132.9 6.9 %collective-permute-start = (bf16[2,512,128]{2,1,0:T(8,128)(2,1)}, bf16[2,512,128]{2,1,0:T(8,128)(2,1)S(1)}, u32[]{:S(2)}, u32[]{:S(2)}) collective-permute-start(bf16[2,512,128]{2,1,0:T(8,128)(2,1)} %get-tuple-element.537), channel_id=1, source_target_pairs={{28,0},{0,4},{4,8},{8,12},{12,16},{16,20},{20,24},{24,28},{29,1},{... | collective-permute-start | bytes 786440 | tf_op jit(solution)/shard_map/while/body/eval_jaxpr/ppermute | solution.py:16
  139.8 5.0 %copy-start.1 = (f32[8,512,128]{2,1,0:T(8,128)S(1)}, f32[8,512,128]{2,1,0:T(8,128)}, u32[]{:S(2)}) copy-start(f32[8,512,128]{2,1,0:T(8,128)} %get-tuple-element.298) | copy-start | bytes 6291460 | tf_op jit(solution)/shard_map/while/body/eval_jaxpr/cond
  148.0 1.3 copy-start.2
  152.8 9.7 %copy-start.5 = (s32[128,8]{0,1:T(8,128)S(1)}, s32[128,8]{0,1:T(8,128)}, u32[]{:S(2)}) copy-start(s32[128,8]{0,1:T(8,128)} %param.21) | copy-start | bytes 12292
  152.8 9.7 %copy-start.6 = (s32[4]{0:T(128)S(1)}, s32[4]{0:T(128)}, u32[]{:S(2)}) copy-start(s32[4]{0:T(128)} %param.22) | copy-start | bytes 52
  152.8 86.7 %copy-start.3 = (bf16[128,4096]{1,0:T(8,128)(2,1)S(1)}, bf16[128,4096]{1,0:T(8,128)(2,1)}, u32[]{:S(2)}) copy-start(bf16[128,4096]{1,0:T(8,128)(2,1)} %param.18) | copy-start | bytes 3145732
  152.8 88.4 %copy-start.7 = (f32[4096]{0:T(1024)S(1)}, f32[4096]{0:T(1024)}, u32[]{:S(2)}) copy-start(f32[4096]{0:T(1024)} %param.20) | copy-start | bytes 49156
  162.5 133.9 %all-gather.2.cloned.1.call-start = ((), (), s32[]{:S(2)}) async-start(), calls=%async_computation.3 | async-start | bytes 4718592 | tf_op jit(solution)/shard_map/all_gather | solution.py:117
  241.2 63.3 %copy-start.4 = (bf16[128,4096]{1,0:T(8,128)(2,1)}, bf16[128,4096]{1,0:T(8,128)(2,1)S(1)}, u32[]{:S(2)}) copy-start(bf16[128,4096]{1,0:T(8,128)(2,1)S(1)} %get-tuple-element.418) | copy-start | bytes 3145732
Sparse Core Ops, SparseCore 0:
  162.6 76.8 reduce-scatter.1
  260.5 35.7 all-gather.1
where the time goes:
time: 314 us; the launch traced here: 311 us
  waiting for transfers between devices  129 us (41%)
  other arithmetic  57.1 us (18%)
  matrix products  56 us (18%)
  local copies, waits for them, and re-layouts  30.9 us (10%)
  blocking collectives  18.6 us (6%)
  between operations  14.9 us (5%)
  loops' own time  4.56 us (1%)
    reduce_scatter x1, waiting for transfers between devices, local(): lax.psum_scatter(jnp.dot(attention, out_weight, preferred_element_type=jn...  76.5 us
    all_gather x1, waiting for transfers between devices, local(): lax.all_gather(arrived, 'ctx', axis=0, tiled=True).reshape(-1, features)  35.9 us
    dot_general x8, matrix products, update(): jnp.einsum('hqk,kd->hqd', unnormed.astype(jnp.bfloat16), pair_now[1], pre...  25.7 us
    all_to_all x1, blocking collectives, local(): lax.all_to_all(outgoing, 'exp', split_axis=0, concat_axis=0, tiled=True)  18.6 us
    add x15, other arithmetic, places(): return block_start * block_len + offsets % block_len  18.6 us
    reduce_sum x8, other arithmetic, update(): new_sum = run_sum * shrink + jnp.sum(unnormed, axis=2)  16.8 us
    ppermute x7, waiting for transfers between devices, from_behind(): return lax.ppermute(block, axis, route)  16 us
    cond x35, local copies, waits for them, and re-layouts  13.4 us
  transfers between devices with their start and end apart: 9, of which 9 were waited for; matrix products, arithmetic and copies ran while one was open for 9% of the time, Pallas kernels for 0%

commit v1 on v0

v1 whole, which is shorter than its diff:
```python
import functools

import jax
import jax.numpy as jnp
from jax import lax
from jax.experimental import pallas as pl
from jax.experimental.pallas import tpu as pltpu
from jax.sharding import PartitionSpec as P

QH = 32
KVH = 2
HD = 128
NE = 128
TOP = 8
LOG2E = 1.4426950408889634
LOW = -1e30


def swap(block, axis, distance):
    count = lax.axis_size(axis)
    return lax.ppermute(block, axis, [(i, i ^ distance) for i in range(count)])


def gather_ctx(block):
    count = lax.axis_size("ctx")
    half = block.shape[0] // 2
    far = [(0, 0, block)]
    if count == 8:
        along_x, along_y = swap(block, "ctx", 2), swap(block, "ctx", 4)
        far += [(2, 0, along_x), (4, 0, along_y)]
        far += [(6, 0, swap(along_y[:half], "ctx", 2)), (6, half, swap(along_x[half:], "ctx", 4))]
    else:
        distance = 2
        while distance < count:
            far += [(d ^ distance, first, swap(b, "ctx", distance)) for d, first, b in far]
            distance *= 2
    return far + [(d ^ 1, first, swap(b, "ctx", 1)) for d, first, b in far]


def attend_kernel(
    start, block_len, slots_ref, place_ref, dest_ref, query_ref, *refs
):
    n_pieces = len(refs) - 6
    pieces, out_ref = refs[:n_pieces], refs[n_pieces]
    key_ref, value_ref, stacked_ref, top_ref, acc_ref = refs[n_pieces + 1:]
    shards, tokens = dest_ref.shape
    rows = out_ref.shape[0] // shards
    heads = out_ref.shape[1] // HD
    shards_half = shards // 2
    half_rows = shards_half * rows
    stack = heads * half_rows
    step_len = 2 * block_len

    slot = 0
    for piece in pieces:
        for part in range(piece.shape[0] // block_len):
            at = pl.ds(pl.multiple_of(slots_ref[slot] * block_len, block_len), block_len)
            block = piece[part * block_len:(part + 1) * block_len, :]
            key_ref[at, :HD] = block[:, :HD]
            key_ref[at, HD:] = block[:, :HD]
            value_ref[at, :HD] = block[:, HD:]
            slot += 1
    value_ref[:, HD:] = jnp.ones((value_ref.shape[0], HD), jnp.bfloat16)

    for half in range(2):
        place = place_ref[half]
        offsets = []
        for s in range(shards_half):
            shard = half * shards_half + s
            picked = dest_ref[shard:shard + 1, :] == start + lax.broadcasted_iota(
                jnp.int32, (rows, tokens), 0
            )
            token = lax.broadcasted_iota(jnp.int32, (rows, tokens), 1)
            offsets.append(
                jnp.sum(jnp.where(picked, token, 0), axis=1, keepdims=True) + s * tokens
            )
            chosen_rows = jnp.dot(
                picked.astype(jnp.bfloat16),
                query_ref[shard * tokens:(shard + 1) * tokens, :],
                preferred_element_type=jnp.float32,
            ) * (LOG2E / HD ** 0.5)
            high = chosen_rows.astype(jnp.bfloat16)
            low = (chosen_rows - high.astype(jnp.float32)).astype(jnp.bfloat16)
            for h in range(heads):
                at = pl.ds(h * half_rows + s * rows, rows)
                stacked_ref[at, :HD] = high[:, h * HD:(h + 1) * HD]
                stacked_ref[at, HD:] = low[:, h * HD:(h + 1) * HD]
        offset = jnp.concatenate(offsets, axis=0)
        query_place = place * block_len + offset
        top_ref[...] = jnp.full(top_ref.shape, LOW, jnp.float32)
        acc_ref[...] = jnp.zeros(acc_ref.shape, jnp.float32)
        tile_heads = max(1, min(heads, 256 // half_rows))
        tile = tile_heads * half_rows

        def absorb(step, masked):
            at = pl.ds(pl.multiple_of(step * step_len, step_len), step_len)
            key_now, value_now = key_ref[at, :], value_ref[at, :]
            if masked:
                key_place = step * step_len + lax.broadcasted_iota(
                    jnp.int32, (half_rows, step_len), 1
                )
                hidden = jnp.where(key_place <= query_place, 0.0, LOW)
                hidden = jnp.concatenate([hidden] * tile_heads, axis=0)
            for t in range(stack // tile):
                here = pl.ds(t * tile, tile)
                scores = lax.dot_general(
                    stacked_ref[here, :], key_now, (((1,), (1,)), ((), ())),
                    preferred_element_type=jnp.float32,
                )
                if masked:
                    scores = scores + hidden
                top = top_ref[here, :]
                new_top = jnp.maximum(top, jnp.max(scores, axis=1, keepdims=True))
                shrink = jnp.exp2(top - new_top)
                unnormed = jnp.exp2(scores - new_top[:, :1]).astype(jnp.bfloat16)
                added = jnp.dot(unnormed, value_now, preferred_element_type=jnp.float32)
                acc_ref[here, :] = acc_ref[here, :] * shrink[:, :1] + added
                top_ref[here, :] = new_top

        lax.fori_loop(0, place // 2, lambda step, _: absorb(step, False), None)
        absorb(place // 2, True)
        for h in range(heads):
            here = pl.ds(h * half_rows, half_rows)
            out_ref[half * half_rows:(half + 1) * half_rows, h * HD:(h + 1) * HD] = (
                acc_ref[here, :HD] / acc_ref[here, HD:]
            ).astype(jnp.bfloat16)


def attend(start, rows, queries, dest, slots, places, pieces, seq):
    shards, tokens = dest.shape
    local_len, width = queries.shape
    block_len = local_len // 2
    half_rows = shards // 2 * rows
    stack = width // HD * half_rows
    smem = pl.BlockSpec(memory_space=pltpu.SMEM)
    vmem = pl.BlockSpec(memory_space=pltpu.VMEM)
    return pl.pallas_call(
        functools.partial(attend_kernel, start, block_len),
        out_shape=jax.ShapeDtypeStruct((shards * rows, width), jnp.bfloat16),
        in_specs=[smem, smem, vmem, vmem] + [vmem] * len(pieces),
        out_specs=vmem,
        scratch_shapes=[
            pltpu.VMEM((seq, 2 * HD), jnp.bfloat16),
            pltpu.VMEM((seq, 2 * HD), jnp.bfloat16),
            pltpu.VMEM((stack, 2 * HD), jnp.bfloat16),
            pltpu.VMEM((stack, HD), jnp.float32),
            pltpu.VMEM((stack, 2 * HD), jnp.float32),
        ],
        compiler_params=pltpu.CompilerParams(vmem_limit_bytes=48 * 1024 * 1024),
        cost_estimate=pl.CostEstimate(
            flops=4 * stack * 2 * seq * HD, bytes_accessed=6 * 1024 * 1024,
            transcendentals=stack * seq,
        ),
    )(slots, places, dest, queries, *pieces)


def scatter_sum(parts_of, column, order):
    bits = len(order)
    keep_axes = {}
    total = None
    for turn, bit in enumerate(order):
        mine = (column >> bit) & 1
        axis = bits - 1 - bit
        if turn == 0:
            send = parts_of(axis, 1 - mine)
            keep = parts_of(axis, mine)
            live = [b for b in range(bits - 1, -1, -1) if b != bit]
        else:
            axis = live.index(bit)
            send = lax.dynamic_index_in_dim(total, 1 - mine, axis, keepdims=False)
            send = send.astype(jnp.bfloat16)
            keep = lax.dynamic_index_in_dim(total, mine, axis, keepdims=False)
            live.remove(bit)
        came = swap(send, "exp", 1 << bit)
        total = keep.astype(jnp.float32) + came.astype(jnp.float32)
    return total


def local(queries, keys, values, residual, out_weight, norm_gain, routes, chosen, block_order):
    ctx_count = lax.axis_size("ctx")
    ctx_rank = lax.axis_index("ctx")
    exp_count = lax.axis_size("exp")
    column = lax.axis_index("exp")
    local_len = queries.shape[0]
    block_len = local_len // 2
    seq = ctx_count * local_len
    heads_here = queries.shape[1] // HD
    token_rows, features = residual.shape
    n_chosen = chosen.shape[0]
    capacity = 2 * token_rows * TOP // NE

    kv_head = column * heads_here // (QH // KVH)
    key_mine = lax.dynamic_slice_in_dim(keys, kv_head * HD, HD, 1)
    value_mine = lax.dynamic_slice_in_dim(values, kv_head * HD, HD, 1)
    gathered = gather_ctx(jnp.concatenate([key_mine, value_mine], axis=1))
    pieces = [piece for _, _, piece in gathered]
    blocks = [
        (distance, first // block_len + part)
        for distance, first, piece in gathered
        for part in range(piece.shape[0] // block_len)
    ]
    owners = jnp.array([distance for distance, _ in blocks], jnp.int32) ^ ctx_rank
    slots = block_order[2 * owners + jnp.array([part for _, part in blocks], jnp.int32)]
    places = lax.dynamic_slice_in_dim(block_order, 2 * ctx_rank, 2, 0)

    routed = jnp.any(routes[:, :, None] == chosen[None, None, :], axis=1)
    named = jnp.any(routed, axis=1).astype(jnp.int32)
    dest = jnp.where(
        named == 1, jnp.cumsum(named) - 1, jnp.sum(named) + jnp.cumsum(1 - named) - 1
    ).astype(jnp.int32)
    shards = dest[None]
    for bit in range(exp_count.bit_length() - 1):
        came = swap(shards, "exp", 1 << bit)
        upper = (column >> bit) & 1
        shards = jnp.where(
            upper == 1, jnp.concatenate([came, shards]), jnp.concatenate([shards, came])
        )
    order = (dest[None, :] == jnp.arange(token_rows, dtype=jnp.int32)[:, None]).astype(
        jnp.bfloat16
    )

    first_rows = min(token_rows, -(-n_chosen * capacity // 16) * 16)
    chunks = [(0, first_rows)]
    if first_rows < token_rows:
        chunks.append((first_rows, token_rows - first_rows))
    bits = exp_count.bit_length() - 1
    residual_ordered = jnp.dot(order, residual, preferred_element_type=jnp.float32)
    half = features // 2
    streams = []
    for start, rows in chunks:
        attention = attend(start, rows, queries, shards, slots, places, pieces, seq)
        attention = attention.reshape((2,) * bits + (rows, heads_here * HD))

        def parts_of(columns, axis, index):
            picked = lax.dynamic_index_in_dim(attention, index, axis, keepdims=False)
            return jnp.einsum(
                "...rk,kd->...rd", picked, out_weight[:, columns * half:(columns + 1) * half],
                preferred_element_type=jnp.float32,
            ).astype(jnp.bfloat16)

        ways = (list(range(bits)), list(range(bits - 1, -1, -1)))
        projection = jnp.concatenate(
            [
                scatter_sum(functools.partial(parts_of, columns), column, ways[columns])
                for columns in range(2)
            ],
            axis=1,
        )
        streams.append((residual_ordered[start:start + rows] + projection).astype(jnp.bfloat16))
    stream = jnp.dot(
        order.T, jnp.concatenate(streams, axis=0), preferred_element_type=jnp.float32
    ).astype(jnp.bfloat16)

    widened = streams[0].astype(jnp.float32)
    normed = (
        widened * lax.rsqrt(jnp.mean(widened * widened, axis=1, keepdims=True) + 1e-06) * norm_gain
    ).astype(jnp.bfloat16)
    arrival = jnp.cumsum(routed.astype(jnp.int32), axis=0) - 1
    slot_ids = jnp.arange(capacity, dtype=jnp.int32)
    placing = (routed.T[:, None, :] & (arrival.T[:, None, :] == slot_ids[None, :, None])).astype(
        jnp.bfloat16
    )
    placing = jnp.einsum(
        "est,rt->esr", placing, order[:first_rows], preferred_element_type=jnp.float32
    ).astype(jnp.bfloat16)
    outgoing = jnp.einsum(
        "esr,rd->esd", placing, normed, preferred_element_type=jnp.float32
    ).astype(jnp.bfloat16)
    arrived = [lax.dynamic_index_in_dim(outgoing, column, 0, keepdims=False)]
    for distance in range(1, exp_count):
        arrived.append(
            swap(
                lax.dynamic_index_in_dim(outgoing, column ^ distance, 0, keepdims=False),
                "exp",
                distance,
            )
        )
    rows_mine = jnp.concatenate(arrived, axis=0)
    every = jnp.concatenate([piece for _, _, piece in gather_ctx(rows_mine)], axis=0)
    rows_dev = features // ctx_count
    own_cols = lax.dynamic_slice_in_dim(every, ctx_rank * rows_dev, rows_dev, 1)
    gram = lax.dot_general(
        own_cols, every, (((0,), (0,)), ((), ())), preferred_element_type=jnp.float32
    )
    mean_rows = seq * TOP // NE
    return (stream, (gram / mean_rows)[None])


def solution(mesh):
    in_specs = (
        P("ctx", "exp"),
        P("ctx", None),
        P("ctx", None),
        P(("ctx", "exp"), None),
        P("exp", None),
        P(),
        P(("ctx", "exp"), None),
        P(),
        P(),
    )
    out_specs = (P(("ctx", "exp"), None), P("exp", "ctx", None))
    return jax.shard_map(local, mesh=mesh, in_specs=in_specs, out_specs=out_specs, check_vma=False)
```

time: 314 us -> 176 us (0.56)
  other arithmetic: 57.1 us -> 6.89 us
  waiting for transfers between devices: 129 us -> 81 us
  Pallas kernels: 0 us -> 44.2 us
  matrix products: 56 us -> 15.3 us
  local copies, waits for them, and re-layouts: 30.9 us -> 3.51 us
  starting transfers between devices: 0.67 us -> 23.7 us
  blocking collectives: 18.6 us -> 0 us
  between operations: 14.9 us -> 1.33 us
  loops' own time: 4.56 us -> 0 us
    reduce_scatter x1 -> x0, waiting for transfers between devices: 76.5 us -> none  [local(): lax.psum_scatter(jnp.dot(attention, out_weight, preferred_element_type=jn...]
    ppermute x7 -> x31, waiting for transfers between devices: 16 us -> 81 us  [swap(): return lax.ppermute(block, axis, [(i, i ^ distance) for i in range(count)])]
    pallas_call x0 -> x2, Pallas kernels: none -> 44.2 us  [attend(): pl.pallas_call(functools.partial(attend_kernel, start, block_len), out_sh...]
    dot_general x19 -> x12, matrix products: 56 us -> 15.3 us  [the longest x1 5.85 us: local(): lax.dot_general(own_cols, every, (((0,), (0,)), ((), ())), preferred_elem...]
    all_gather x1 -> x0, waiting for transfers between devices: 35.9 us -> none  [local(): lax.all_gather(arrived, 'ctx', axis=0, tiled=True).reshape(-1, features)]
    add x23 -> x4, other arithmetic: 24.5 us -> 0.2 us  [scatter_sum(): total = keep.astype(jnp.float32) + came.astype(jnp.float32)]
    ppermute x7 -> x31, starting transfers between devices: 0.59 us -> 23.7 us  [swap(): return lax.ppermute(block, axis, [(i, i ^ distance) for i in range(count)])]
    all_to_all x1 -> x0, blocking collectives: 18.6 us -> none  [local(): lax.all_to_all(outgoing, 'exp', split_axis=0, concat_axis=0, tiled=True)]
  transfers between devices with their start and end apart: 9 -> 31, of which waited for: 9 -> 17; matrix products, arithmetic and copies ran while one was open for 9% -> 9% of each run, Pallas kernels for 0% -> 0%
where the time goes in v1:
time: 176 us
  waiting for transfers between devices  81 us (46%)
  Pallas kernels  44.2 us (25%)
  starting transfers between devices  23.7 us (13%)
  matrix products  15.3 us (9%)
  other arithmetic  6.89 us (4%)
  local copies, waits for them, and re-layouts  3.51 us (2%)
    ppermute x31, waiting for transfers between devices, swap(): return lax.ppermute(block, axis, [(i, i ^ distance) for i in range(count)])  81 us
    pallas_call x2, Pallas kernels, attend(): pl.pallas_call(functools.partial(attend_kernel, start, block_len), out_sh...  44.2 us
    ppermute x31, starting transfers between devices, swap(): return lax.ppermute(block, axis, [(i, i ^ distance) for i in range(count)])  23.7 us
    dot_general x1, matrix products, local(): lax.dot_general(own_cols, every, (((0,), (0,)), ((), ())), preferred_elem...  5.85 us
    dot_general x8, matrix products, parts_of(): jnp.einsum('...rk,kd->...rd', picked, out_weight[:, columns * half:(colum...  5.84 us
  transfers between devices with their start and end apart: 31, of which 17 were waited for; matrix products, arithmetic and copies ran while one was open for 9% of the time, Pallas kernels for 0%

profile of v1, /device:TPU:0, one launch (start us, length us, event | category | flops | bytes accessed | tf_op | source)
XLA Modules:
  0.0 176.0 jit_solution(834808801570227000)
XLA Ops:
  0.7 1.1 constant_dynamic-slice_fusion
  1.9 0.5 collective-permute-start.6
  2.4 2.6 %collective-permute-start.3 = (bf16[512,256]{1,0:T(8,128)(2,1)S(1)}, bf16[512,256]{1,0:T(8,128)(2,1)S(1)}, u32[]{:S(2)}, u32[]{:S(2)}) collective-permute-start(bf16[512,256]{1,0:T(8,128)(2,1)S(1)} %pad_maximum_fusion.1.refs_0_), channel_id=1, source_target_pairs={{0,16},{4,20},{8,24},{12,28},{16,0},{20,4},{24,8},{28,12},{1,17},{... | collective-permute-start | bytes 786440 | tf_op jit(solution)/shard_map/ppermute | solution.py:21
  5.0 1.5 collective-permute-start.2
  6.5 0.8 compare_reduce_fusion
  7.3 0.6 convert_reduce_fusion
  7.9 0.3 reduce-window_1_clone.1
  8.2 0.3 reduce-window_clone.1
  8.5 0.6 compare_select_fusion.1
  9.2 1.6 collective-permute-start
  10.8 0.6 compare_select_fusion.2
  11.6 0.2 reduce_window_sum.20
  11.8 1.7 fusion.105
  13.5 0.6 add_bitcast_fusion
  14.2 2.7 %collective-permute-start.1 = (s32[2,128]{1,0:T(2,128)S(1)}, s32[2,128]{1,0:T(2,128)S(1)}, u32[]{:S(2)}, u32[]{:S(2)}) collective-permute-start(s32[2,128]{1,0:T(2,128)S(1)} %add_select_fusion.1), channel_id=1, source_target_pairs={{0,2},{1,3},{2,0},{3,1},{4,6},{5,7},{6,4},{7,5},{8,10},{9,11},{10,... | collective-permute-start | bytes 3080 | tf_op jit(solution)/shard_map/ppermute | solution.py:21
  16.8 0.6 iota_compare_fusion
  17.5 0.6 collective-permute-start.4
  18.1 0.6 collective-permute-start.5
  18.7 0.5 collective-permute-start.7
  19.2 0.7 compare_select_fusion
  19.9 2.7 %collective-permute-done.4.refs_3_ = bf16[256,256]{1,0:T(8,128)(2,1)S(1)} collective-permute-done((bf16[256,256]{1,0:T(8,128)(2,1)S(1)}, bf16[256,256]{1,0:T(8,128)(2,1)S(1)}, u32[]{:S(2)}, u32[]{:S(2)}) %collective-permute-start.4) | collective-permute-done | bytes 131104 | tf_op jit(solution)/shard_map/ppermute | solution.py:21
  22.5 0.7 collective-permute-done.5.refs_4_
  23.4 0.7 gather_fusion
  24.0 0.9 copy.20
  25.0 0.9 add_select_fusion.dest_ref
  25.9 22.2 %shard_map.123 = bf16[256,1024]{1,0:T(8,128)(2,1)S(1)} custom-call(s32[16]{0:T(128)S(1)} %gather_fusion, s32[2]{0:T(128)S(1)} %dynamic_slice.76.place_ref, s32[4,128]{1,0:T(4,128)S(1)} %add_select_fusion.dest_ref, bf16[512,1024]{1,0:T(8,128)(2,1)S(1)} %copy-done.1, bf16[512,256]{1,0:T(8,128)(2,1)S(1)} %pad_maximum_fusion.1.refs_0_, ...), custom_call_target="tpu_custom_call" | custom-call | flops 4294967296 | bytes 6291456 | tf_op jit(solution)/shard_map/pallas_call | solution.py:137
  48.2 0.7 fusion.45
  48.9 22.0 %shard_map.122 = bf16[256,1024]{1,0:T(8,128)(2,1)S(1)} custom-call(s32[16]{0:T(128)S(1)} %gather_fusion, s32[2]{0:T(128)S(1)} %dynamic_slice.76.place_ref, s32[4,128]{1,0:T(4,128)S(1)} %add_select_fusion.dest_ref, bf16[512,1024]{1,0:T(8,128)(2,1)S(1)} %copy-done.1, bf16[512,256]{1,0:T(8,128)(2,1)S(1)} %pad_maximum_fusion.1.refs_0_, ...), custom_call_target="tpu_custom_call" | custom-call | flops 4294967296 | bytes 6291456 | tf_op jit(solution)/shard_map/pallas_call | solution.py:137
  70.9 0.7 fusion.33
  71.6 0.5 collective-permute-start.11
  72.1 0.7 fusion.57
  72.9 0.4 collective-permute-start.13
  73.3 1.6 collective-permute-start.15
  74.8 0.7 fusion.69
  75.6 2.6 %collective-permute-start.17 = (bf16[2,64,2048]{2,1,0:T(8,128)(2,1)S(1)}, bf16[2,64,2048]{2,1,0:T(8,128)(2,1)S(1)}, u32[]{:S(2)}, u32[]{:S(2)}) collective-permute-start(bf16[2,64,2048]{2,1,0:T(8,128)(2,1)S(1)} %fusion.69), channel_id=1, source_target_pairs={{0,2},{1,3},{2,0},{3,1},{4,6},{5,7},{6,4},{7,5},{8,10},{9,11},{10,... | collective-permute-start | bytes 1572872 | tf_op jit(solution)/shard_map/ppermute | solution.py:21
  78.2 15.2 %collective-permute-done.11 = bf16[2,64,2048]{2,1,0:T(8,128)(2,1)S(1)} collective-permute-done((bf16[2,64,2048]{2,1,0:T(8,128)(2,1)S(1)}, bf16[2,64,2048]{2,1,0:T(8,128)(2,1)S(1)}, u32[]{:S(2)}, u32[]{:S(2)}) %collective-permute-start.11) | collective-permute-done | bytes 524320 | tf_op jit(solution)/shard_map/ppermute | solution.py:21
  93.5 0.7 fusion.30
  94.3 9.5 %collective-permute-done.13 = bf16[2,64,2048]{2,1,0:T(8,128)(2,1)S(1)} collective-permute-done((bf16[2,64,2048]{2,1,0:T(8,128)(2,1)S(1)}, bf16[2,64,2048]{2,1,0:T(8,128)(2,1)S(1)}, u32[]{:S(2)}, u32[]{:S(2)}) %collective-permute-start.13) | collective-permute-done | bytes 524320 | tf_op jit(solution)/shard_map/ppermute | solution.py:21
  103.8 0.7 fusion.54
  104.7 7.2 %collective-permute-done.15 = bf16[2,64,2048]{2,1,0:T(8,128)(2,1)S(1)} collective-permute-done((bf16[2,64,2048]{2,1,0:T(8,128)(2,1)S(1)}, bf16[2,64,2048]{2,1,0:T(8,128)(2,1)S(1)}, u32[]{:S(2)}, u32[]{:S(2)}) %collective-permute-start.15) | collective-permute-done | bytes 524320 | tf_op jit(solution)/shard_map/ppermute | solution.py:21
  111.9 0.8 fusion.42
  112.7 10.8 %collective-permute-done.17 = bf16[2,64,2048]{2,1,0:T(8,128)(2,1)S(1)} collective-permute-done((bf16[2,64,2048]{2,1,0:T(8,128)(2,1)S(1)}, bf16[2,64,2048]{2,1,0:T(8,128)(2,1)S(1)}, u32[]{:S(2)}, u32[]{:S(2)}) %collective-permute-start.17) | collective-permute-done | bytes 524320 | tf_op jit(solution)/shard_map/ppermute | solution.py:21
  123.6 0.8 fusion.66
  124.5 5.6 %collective-permute-done.12 = bf16[64,2048]{1,0:T(8,128)(2,1)S(1)} collective-permute-done((bf16[64,2048]{1,0:T(8,128)(2,1)S(1)}, bf16[64,2048]{1,0:T(8,128)(2,1)S(1)}, u32[]{:S(2)}, u32[]{:S(2)}) %collective-permute-start.12) | collective-permute-done | bytes 262176 | tf_op jit(solution)/shard_map/ppermute | solution.py:21
  130.2 2.7 %collective-permute-done.16 = bf16[64,2048]{1,0:T(8,128)(2,1)S(1)} collective-permute-done((bf16[64,2048]{1,0:T(8,128)(2,1)S(1)}, bf16[64,2048]{1,0:T(8,128)(2,1)S(1)}, u32[]{:S(2)}, u32[]{:S(2)}) %collective-permute-start.16) | collective-permute-done | bytes 262176 | tf_op jit(solution)/shard_map/ppermute | solution.py:21
  132.9 2.6 %collective-permute-done.18 = bf16[64,2048]{1,0:T(8,128)(2,1)S(1)} collective-permute-done((bf16[64,2048]{1,0:T(8,128)(2,1)S(1)}, bf16[64,2048]{1,0:T(8,128)(2,1)S(1)}, u32[]{:S(2)}, u32[]{:S(2)}) %collective-permute-start.18) | collective-permute-done | bytes 262176 | tf_op jit(solution)/shard_map/ppermute | solution.py:21
  135.7 0.3 fusion.72
  136.0 0.4 convolution_convert_fusion.1
  136.5 0.6 collective-permute-start.21
  137.1 0.4 collective-permute-start.20
  137.6 3.4 %collective-permute-start.19 = (bf16[16,4096]{1,0:T(8,128)(2,1)S(1)}, bf16[16,4096]{1,0:T(8,128)(2,1)S(1)}, u32[]{:S(2)}, u32[]{:S(2)}) collective-permute-start(bf16[16,4096]{1,0:T(8,128)(2,1)S(1)} %get-tuple-element.11), channel_id=1, source_target_pairs={{0,1},{1,0},{2,3},{3,2},{4,5},{5,4},{6,7},{7,6},{8,9},{9,8},{10,11... | collective-permute-start | bytes 393224 | tf_op jit(solution)/shard_map/ppermute | solution.py:21
  141.0 1.5 convolution_convert_fusion
  142.4 1.1 collective-permute-done.21
  143.5 2.3 %collective-permute-done.20 = bf16[16,4096]{1,0:T(8,128)(2,1)S(1)} collective-permute-done((bf16[16,4096]{1,0:T(8,128)(2,1)S(1)}, bf16[16,4096]{1,0:T(8,128)(2,1)S(1)}, u32[]{:S(2)}, u32[]{:S(2)}) %collective-permute-start.20) | collective-permute-done | bytes 131104 | tf_op jit(solution)/shard_map/ppermute | solution.py:21
  145.9 0.8 collective-permute-start.23
  146.8 13.5 %collective-permute-done.23 = bf16[64,4096]{1,0:T(8,128)(2,1)S(1)} collective-permute-done((bf16[64,4096]{1,0:T(8,128)(2,1)S(1)}, bf16[64,4096]{1,0:T(8,128)(2,1)S(1)}, u32[]{:S(2)}, u32[]{:S(2)}) %collective-permute-start.23) | collective-permute-done | bytes 524320 | tf_op jit(solution)/shard_map/ppermute | solution.py:21
  160.4 0.3 collective-permute-done.22
  160.7 1.4 collective-permute-start.25
  162.1 0.5 collective-permute-start.27
  162.7 5.5 %collective-permute-done.24 = bf16[32,4096]{1,0:T(8,128)(2,1)S(1)} collective-permute-done((bf16[32,4096]{1,0:T(8,128)(2,1)S(1)}, bf16[32,4096]{1,0:T(8,128)(2,1)S(1)}, u32[]{:S(2)}, u32[]{:S(2)}) %collective-permute-start.24) | collective-permute-done | bytes 262176 | tf_op jit(solution)/shard_map/ppermute | solution.py:21
  168.4 0.5 collective-permute-start.30
  169.0 0.7 collective-permute-done.29
  169.8 0.4 collective-permute-done.30
  170.2 5.8 %multiply_bitcast_fusion = f32[1,512,4096]{2,1,0:T(8,128)} fusion(bf16[512,4096]{1,0:T(8,128)(2,1)S(1)} %constant_dynamic-update-slice_fusion, s32[]{:T(128)S(6)} %select_n.106), kind=kOutput, calls=%fused_computation.1 | convolution fusion | flops 2149580800 | bytes 13107204 | tf_op jit(solution)/shard_map/dot_general | solution.py:282
  (99 shorter events, 1.7 us)
Async XLA Ops:
  0.6 11.2 %copy-start = (bf16[128,4096]{1,0:T(8,128)(2,1)S(1)}, bf16[128,4096]{1,0:T(8,128)(2,1)}, u32[]{:S(2)}) copy-start(bf16[128,4096]{1,0:T(8,128)(2,1)} %param.14) | copy-start | bytes 3145732
  0.6 18.5 %copy-start.12 = (s32[16]{0:T(128)S(1)}, s32[16]{0:T(128)}, u32[]{:S(2)}) copy-start(s32[16]{0:T(128)} %constant.124.clone) | copy-start | bytes 196
  0.7 22.6 %copy-start.2 = (s32[16]{0:T(128)S(1)}, s32[16]{0:T(128)}, u32[]{:S(2)}) copy-start(s32[16]{0:T(128)} %param.19) | copy-start | bytes 196
  0.7 25.2 %copy-start.1 = (bf16[512,1024]{1,0:T(8,128)(2,1)S(1)}, bf16[512,1024]{1,0:T(8,128)(2,1)}, u32[]{:S(2)}) copy-start(bf16[512,1024]{1,0:T(8,128)(2,1)} %query_ref.3) | copy-start | bytes 3145732
  1.9 24.0 %collective-permute-start.6 = (bf16[512,256]{1,0:T(8,128)(2,1)S(1)}, bf16[512,256]{1,0:T(8,128)(2,1)S(1)}, u32[]{:S(2)}, u32[]{:S(2)}) collective-permute-start(bf16[512,256]{1,0:T(8,128)(2,1)S(1)} %pad_maximum_fusion.1.refs_0_), channel_id=1, source_target_pairs={{0,4},{4,0},{8,12},{12,8},{16,20},{20,16},{24,28},{28,24},{1,5},{5... | collective-permute-start | bytes 786440 | tf_op jit(solution)/shard_map/ppermute | solution.py:21
  2.4 15.1 %collective-permute-start.3 = (bf16[512,256]{1,0:T(8,128)(2,1)S(1)}, bf16[512,256]{1,0:T(8,128)(2,1)S(1)}, u32[]{:S(2)}, u32[]{:S(2)}) collective-permute-start(bf16[512,256]{1,0:T(8,128)(2,1)S(1)} %pad_maximum_fusion.1.refs_0_), channel_id=1, source_target_pairs={{0,16},{4,20},{8,24},{12,28},{16,0},{20,4},{24,8},{28,12},{1,17},{... | collective-permute-start | bytes 786440 | tf_op jit(solution)/shard_map/ppermute | solution.py:21
  5.0 13.1 %collective-permute-start.2 = (bf16[512,256]{1,0:T(8,128)(2,1)S(1)}, bf16[512,256]{1,0:T(8,128)(2,1)S(1)}, u32[]{:S(2)}, u32[]{:S(2)}) collective-permute-start(bf16[512,256]{1,0:T(8,128)(2,1)S(1)} %pad_maximum_fusion.1.refs_0_), channel_id=1, source_target_pairs={{0,8},{4,12},{8,0},{12,4},{16,24},{20,28},{24,16},{28,20},{1,9},{5... | collective-permute-start | bytes 786440 | tf_op jit(solution)/shard_map/ppermute | solution.py:21
  7.3 4.2 %copy-start.8 = (pred[128,4]{0,1:T(4,128)(4,1)}, pred[128,4]{0,1:T(4,128)(4,1)S(1)}, u32[]{:S(2)}) copy-start(pred[128,4]{0,1:T(4,128)(4,1)S(1)} %get-tuple-element.2) | copy-start | bytes 1540
  9.2 5.0 %collective-permute-start = (s32[1,128]{1,0:T(1,128)S(1)}, s32[1,128]{1,0:T(1,128)S(1)}, u32[]{:S(2)}, u32[]{:S(2)}) collective-permute-start(s32[1,128]{1,0:T(1,128)S(1)} %compare_select_fusion.1), channel_id=1, source_target_pairs={{0,1},{1,0},{2,3},{3,2},{4,5},{5,4},{6,7},{7,6},{8,9},{9,8},{10,11... | collective-permute-start | bytes 1544 | tf_op jit(solution)/shard_map/ppermute | solution.py:21
  11.5 6.6 %copy-start.6 = (s32[128]{0:T(128)}, s32[128]{0:T(128)S(1)}, u32[]{:S(2)}) copy-start(s32[128]{0:T(128)S(1)} %compare_select_fusion.2) | copy-start | bytes 1540
  14.2 9.1 %copy-start.10 = (s32[2,128]{1,0:T(2,128)}, s32[2,128]{1,0:T(2,128)S(1)}, u32[]{:S(2)}) copy-start(s32[2,128]{1,0:T(2,128)S(1)} %add_select_fusion.1) | copy-start | bytes 3076
  14.2 4.5 %collective-permute-start.1 = (s32[2,128]{1,0:T(2,128)S(1)}, s32[2,128]{1,0:T(2,128)S(1)}, u32[]{:S(2)}, u32[]{:S(2)}) collective-permute-start(s32[2,128]{1,0:T(2,128)S(1)} %add_select_fusion.1), channel_id=1, source_target_pairs={{0,2},{1,3},{2,0},{3,1},{4,6},{5,7},{6,4},{7,5},{8,10},{9,11},{10,... | collective-permute-start | bytes 3080 | tf_op jit(solution)/shard_map/ppermute | solution.py:21
  17.5 5.0 %collective-permute-start.4 = (bf16[256,256]{1,0:T(8,128)(2,1)S(1)}, bf16[256,256]{1,0:T(8,128)(2,1)S(1)}, u32[]{:S(2)}, u32[]{:S(2)}) collective-permute-start(bf16[256,256]{1,0:T(8,128)(2,1)S(1)} %slice.45), channel_id=1, source_target_pairs={{0,8},{4,12},{8,0},{12,4},{16,24},{20,28},{24,16},{28,20},{1,9},{5... | collective-permute-start | bytes 393224 | tf_op jit(solution)/shard_map/ppermute | solution.py:21
  18.1 5.1 %collective-permute-start.5 = (bf16[256,256]{1,0:T(8,128)(2,1)S(1)}, bf16[256,256]{1,0:T(8,128)(2,1)}, u32[]{:S(2)}, u32[]{:S(2)}) collective-permute-start(bf16[256,256]{1,0:T(8,128)(2,1)S(1)} %slice.46), channel_id=1, source_target_pairs={{0,16},{4,20},{8,24},{12,28},{16,0},{20,4},{24,8},{28,12},{1,17},{... | collective-permute-start | bytes 393224 | tf_op jit(solution)/shard_map/ppermute | solution.py:21
  18.7 7.2 %collective-permute-start.8 = (bf16[512,256]{1,0:T(8,128)(2,1)S(1)}, bf16[512,256]{1,0:T(8,128)(2,1)S(1)}, u32[]{:S(2)}, u32[]{:S(2)}) collective-permute-start(bf16[512,256]{1,0:T(8,128)(2,1)S(1)} %collective-permute-done.3.refs_2_), channel_id=1, source_target_pairs={{0,4},{4,0},{8,12},{12,8},{16,20},{20,16},{24,28},{28,24},{1,5},{5... | collective-permute-start | bytes 786440 | tf_op jit(solution)/shard_map/ppermute | solution.py:21
  18.7 4.6 %copy-start.11 = (s32[2,128]{1,0:T(2,128)}, s32[2,128]{1,0:T(2,128)S(1)}, u32[]{:S(2)}) copy-start(s32[2,128]{1,0:T(2,128)S(1)} %collective-permute-done.1) | copy-start | bytes 3076
  18.7 7.2 %collective-permute-start.7 = (bf16[512,256]{1,0:T(8,128)(2,1)S(1)}, bf16[512,256]{1,0:T(8,128)(2,1)}, u32[]{:S(2)}, u32[]{:S(2)}) collective-permute-start(bf16[512,256]{1,0:T(8,128)(2,1)S(1)} %collective-permute-done.2.refs_1_), channel_id=1, source_target_pairs={{0,4},{4,0},{8,12},{12,8},{16,20},{20,16},{24,28},{28,24},{1,5},{5... | collective-permute-start | bytes 786440 | tf_op jit(solution)/shard_map/ppermute | solution.py:21
  22.5 3.3 %collective-permute-start.9 = (bf16[256,256]{1,0:T(8,128)(2,1)S(1)}, bf16[256,256]{1,0:T(8,128)(2,1)}, u32[]{:S(2)}, u32[]{:S(2)}) collective-permute-start(bf16[256,256]{1,0:T(8,128)(2,1)S(1)} %collective-permute-done.4.refs_3_), channel_id=1, source_target_pairs={{0,4},{4,0},{8,12},{12,8},{16,20},{20,16},{24,28},{28,24},{1,5},{5... | collective-permute-start | bytes 393224 | tf_op jit(solution)/shard_map/ppermute | solution.py:21
  23.2 2.6 %collective-permute-start.10 = (bf16[256,256]{1,0:T(8,128)(2,1)}, bf16[256,256]{1,0:T(8,128)(2,1)}, u32[]{:S(2)}, u32[]{:S(2)}) collective-permute-start(bf16[256,256]{1,0:T(8,128)(2,1)} %collective-permute-done.5.refs_4_), channel_id=1, source_target_pairs={{0,4},{4,0},{8,12},{12,8},{16,20},{20,16},{24,28},{28,24},{1,5},{5... | collective-permute-start | bytes 393224 | tf_op jit(solution)/shard_map/ppermute | solution.py:21
  24.9 23.2 %slice-start = ((s8[8388608]{0:T(1024)(128)(4,1)}), s8[4194304]{0:T(1024)(128)(4,1)S(1)}, s32[]{:S(2)}) async-start(s8[8388608]{0:T(1024)(128)(4,1)} %bitcast.134), calls=%async_computation | async-start | bytes 8388608
  25.8 22.3 %slice-start.1 = ((s8[8388608]{0:T(1024)(128)(4,1)}), s8[4194304]{0:T(1024)(128)(4,1)S(1)}, s32[]{:S(2)}) async-start(s8[8388608]{0:T(1024)(128)(4,1)} %bitcast.134), calls=%async_computation.1 | async-start | bytes 8388608
  71.6 21.9 %collective-permute-start.11 = (bf16[2,64,2048]{2,1,0:T(8,128)(2,1)S(1)}, bf16[2,64,2048]{2,1,0:T(8,128)(2,1)S(1)}, u32[]{:S(2)}, u32[]{:S(2)}) collective-permute-start(bf16[2,64,2048]{2,1,0:T(8,128)(2,1)S(1)} %fusion.33), channel_id=1, source_target_pairs={{0,1},{1,0},{2,3},{3,2},{4,5},{5,4},{6,7},{7,6},{8,9},{9,8},{10,11... | collective-permute-start | bytes 1572872 | tf_op jit(solution)/shard_map/ppermute | solution.py:21
  72.9 31.0 %collective-permute-start.13 = (bf16[2,64,2048]{2,1,0:T(8,128)(2,1)S(1)}, bf16[2,64,2048]{2,1,0:T(8,128)(2,1)S(1)}, u32[]{:S(2)}, u32[]{:S(2)}) collective-permute-start(bf16[2,64,2048]{2,1,0:T(8,128)(2,1)S(1)} %fusion.57), channel_id=1, source_target_pairs={{0,2},{1,3},{2,0},{3,1},{4,6},{5,7},{6,4},{7,5},{8,10},{9,11},{10,... | collective-permute-start | bytes 1572872 | tf_op jit(solution)/shard_map/ppermute | solution.py:21
  73.3 38.6 %collective-permute-start.15 = (bf16[2,64,2048]{2,1,0:T(8,128)(2,1)S(1)}, bf16[2,64,2048]{2,1,0:T(8,128)(2,1)S(1)}, u32[]{:S(2)}, u32[]{:S(2)}) collective-permute-start(bf16[2,64,2048]{2,1,0:T(8,128)(2,1)S(1)} %fusion.45), channel_id=1, source_target_pairs={{0,1},{1,0},{2,3},{3,2},{4,5},{5,4},{6,7},{7,6},{8,9},{9,8},{10,11... | collective-permute-start | bytes 1572872 | tf_op jit(solution)/shard_map/ppermute | solution.py:21
  75.6 48.0 %collective-permute-start.17 = (bf16[2,64,2048]{2,1,0:T(8,128)(2,1)S(1)}, bf16[2,64,2048]{2,1,0:T(8,128)(2,1)S(1)}, u32[]{:S(2)}, u32[]{:S(2)}) collective-permute-start(bf16[2,64,2048]{2,1,0:T(8,128)(2,1)S(1)} %fusion.69), channel_id=1, source_target_pairs={{0,2},{1,3},{2,0},{3,1},{4,6},{5,7},{6,4},{7,5},{8,10},{9,11},{10,... | collective-permute-start | bytes 1572872 | tf_op jit(solution)/shard_map/ppermute | solution.py:21
  94.2 35.8 %collective-permute-start.12 = (bf16[64,2048]{1,0:T(8,128)(2,1)S(1)}, bf16[64,2048]{1,0:T(8,128)(2,1)S(1)}, u32[]{:S(2)}, u32[]{:S(2)}) collective-permute-start(bf16[64,2048]{1,0:T(8,128)(2,1)S(1)} %fusion.85), channel_id=1, source_target_pairs={{0,2},{1,3},{2,0},{3,1},{4,6},{5,7},{6,4},{7,5},{8,10},{9,11},{10,... | collective-permute-start | bytes 786440 | tf_op jit(solution)/shard_map/ppermute | solution.py:21
  103.8 19.7 %slice-start.2 = ((s8[8388608]{0:T(1024)(128)(4,1)}), s8[4194304]{0:T(1024)(128)(4,1)S(1)}, s32[]{:S(2)}) async-start(s8[8388608]{0:T(1024)(128)(4,1)} %bitcast.136), calls=%async_computation.2 | async-start | bytes 8388608
  104.6 19.0 %slice-start.3 = ((s8[8388608]{0:T(1024)(128)(4,1)}), s8[4194304]{0:T(1024)(128)(4,1)S(1)}, s32[]{:S(2)}) async-start(s8[8388608]{0:T(1024)(128)(4,1)} %bitcast.136), calls=%async_computation.3 | async-start | bytes 8388608
  104.6 25.5 %collective-permute-start.14 = (bf16[64,2048]{1,0:T(8,128)(2,1)S(1)}, bf16[64,2048]{1,0:T(8,128)(2,1)S(1)}, u32[]{:S(2)}, u32[]{:S(2)}) collective-permute-start(bf16[64,2048]{1,0:T(8,128)(2,1)S(1)} %fusion.86), channel_id=1, source_target_pairs={{0,1},{1,0},{2,3},{3,2},{4,5},{5,4},{6,7},{7,6},{8,9},{9,8},{10,11... | collective-permute-start | bytes 786440 | tf_op jit(solution)/shard_map/ppermute | solution.py:21
  112.7 20.2 %collective-permute-start.16 = (bf16[64,2048]{1,0:T(8,128)(2,1)S(1)}, bf16[64,2048]{1,0:T(8,128)(2,1)S(1)}, u32[]{:S(2)}, u32[]{:S(2)}) collective-permute-start(bf16[64,2048]{1,0:T(8,128)(2,1)S(1)} %fusion.87), channel_id=1, source_target_pairs={{0,2},{1,3},{2,0},{3,1},{4,6},{5,7},{6,4},{7,5},{8,10},{9,11},{10,... | collective-permute-start | bytes 786440 | tf_op jit(solution)/shard_map/ppermute | solution.py:21
  124.3 11.3 %copy-start.3 = (f32[128,4096]{1,0:T(8,128)S(1)}, f32[128,4096]{1,0:T(8,128)}, u32[]{:S(2)}) copy-start(f32[128,4096]{1,0:T(8,128)} %fusion.105) | copy-start | bytes 6291460
  124.4 11.2 %collective-permute-start.18 = (bf16[64,2048]{1,0:T(8,128)(2,1)S(1)}, bf16[64,2048]{1,0:T(8,128)(2,1)S(1)}, u32[]{:S(2)}, u32[]{:S(2)}) collective-permute-start(bf16[64,2048]{1,0:T(8,128)(2,1)S(1)} %fusion.88), channel_id=1, source_target_pairs={{0,1},{1,0},{2,3},{3,2},{4,5},{5,4},{6,7},{7,6},{8,9},{9,8},{10,11... | collective-permute-start | bytes 786440 | tf_op jit(solution)/shard_map/ppermute | solution.py:21
  130.2 5.8 %copy-start.4 = (pred[128,128]{1,0:T(32,128)(4,1)S(1)}, pred[128,128]{1,0:T(32,128)(4,1)}, u32[]{:S(2)}) copy-start(pred[128,128]{1,0:T(32,128)(4,1)} %iota_compare_fusion) | copy-start | bytes 49156
  130.2 5.8 %copy-start.5 = (f32[4096]{0:T(1024)S(1)}, f32[4096]{0:T(1024)}, u32[]{:S(2)}) copy-start(f32[4096]{0:T(1024)} %param.16) | copy-start | bytes 49156
  130.2 5.8 %copy-start.9 = (pred[128,4]{0,1:T(4,128)(4,1)S(1)}, pred[128,4]{0,1:T(4,128)(4,1)}, u32[]{:S(2)}) copy-start(pred[128,4]{0,1:T(4,128)(4,1)} %copy-done.8) | copy-start | bytes 1540
  132.9 8.0 %copy-start.7 = (s32[128]{0:T(128)S(1)}, s32[128]{0:T(128)}, u32[]{:S(2)}) copy-start(s32[128]{0:T(128)} %copy-done.6) | copy-start | bytes 1540
  136.5 7.0 %collective-permute-start.21 = (bf16[16,4096]{1,0:T(8,128)(2,1)S(1)}, bf16[16,4096]{1,0:T(8,128)(2,1)S(1)}, u32[]{:S(2)}, u32[]{:S(2)}) collective-permute-start(bf16[16,4096]{1,0:T(8,128)(2,1)S(1)} %get-tuple-element.9), channel_id=1, source_target_pairs={{0,3},{1,2},{2,1},{3,0},{4,7},{5,6},{6,5},{7,4},{8,11},{9,10},{10,... | collective-permute-start | bytes 393224 | tf_op jit(solution)/shard_map/ppermute | solution.py:21
  137.1 8.7 %collective-permute-start.20 = (bf16[16,4096]{1,0:T(8,128)(2,1)S(1)}, bf16[16,4096]{1,0:T(8,128)(2,1)S(1)}, u32[]{:S(2)}, u32[]{:S(2)}) collective-permute-start(bf16[16,4096]{1,0:T(8,128)(2,1)S(1)} %get-tuple-element.10), channel_id=1, source_target_pairs={{0,2},{1,3},{2,0},{3,1},{4,6},{5,7},{6,4},{7,5},{8,10},{9,11},{10,... | collective-permute-start | bytes 393224 | tf_op jit(solution)/shard_map/ppermute | solution.py:21
  137.6 8.3 %collective-permute-start.19 = (bf16[16,4096]{1,0:T(8,128)(2,1)S(1)}, bf16[16,4096]{1,0:T(8,128)(2,1)S(1)}, u32[]{:S(2)}, u32[]{:S(2)}) collective-permute-start(bf16[16,4096]{1,0:T(8,128)(2,1)S(1)} %get-tuple-element.11), channel_id=1, source_target_pairs={{0,1},{1,0},{2,3},{3,2},{4,5},{5,4},{6,7},{7,6},{8,9},{9,8},{10,11... | collective-permute-start | bytes 393224 | tf_op jit(solution)/shard_map/ppermute | solution.py:21
  145.9 23.0 %collective-permute-start.26 = (bf16[64,4096]{1,0:T(8,128)(2,1)S(1)}, bf16[64,4096]{1,0:T(8,128)(2,1)S(1)}, u32[]{:S(2)}, u32[]{:S(2)}) collective-permute-start(bf16[64,4096]{1,0:T(8,128)(2,1)S(1)} %pad_maximum_fusion), channel_id=1, source_target_pairs={{0,4},{4,0},{8,12},{12,8},{16,20},{20,16},{24,28},{28,24},{1,5},{5... | collective-permute-start | bytes 1572872 | tf_op jit(solution)/shard_map/ppermute | solution.py:21
  145.9 14.3 %collective-permute-start.23 = (bf16[64,4096]{1,0:T(8,128)(2,1)S(1)}, bf16[64,4096]{1,0:T(8,128)(2,1)S(1)}, u32[]{:S(2)}, u32[]{:S(2)}) collective-permute-start(bf16[64,4096]{1,0:T(8,128)(2,1)S(1)} %pad_maximum_fusion), channel_id=1, source_target_pairs={{0,16},{4,20},{8,24},{12,28},{16,0},{20,4},{24,8},{28,12},{1,17},{... | collective-permute-start | bytes 1572872 | tf_op jit(solution)/shard_map/ppermute | solution.py:21
  146.7 14.0 %collective-permute-start.22 = (bf16[64,4096]{1,0:T(8,128)(2,1)S(1)}, bf16[64,4096]{1,0:T(8,128)(2,1)S(1)}, u32[]{:S(2)}, u32[]{:S(2)}) collective-permute-start(bf16[64,4096]{1,0:T(8,128)(2,1)S(1)} %pad_maximum_fusion), channel_id=1, source_target_pairs={{0,8},{4,12},{8,0},{12,4},{16,24},{20,28},{24,16},{28,20},{1,9},{5... | collective-permute-start | bytes 1572872 | tf_op jit(solution)/shard_map/ppermute | solution.py:21
  160.3 7.9 %collective-permute-start.24 = (bf16[32,4096]{1,0:T(8,128)(2,1)S(1)}, bf16[32,4096]{1,0:T(8,128)(2,1)S(1)}, u32[]{:S(2)}, u32[]{:S(2)}) collective-permute-start(bf16[32,4096]{1,0:T(8,128)(2,1)S(1)} %slice.49), channel_id=1, source_target_pairs={{0,8},{4,12},{8,0},{12,4},{16,24},{20,28},{24,16},{28,20},{1,9},{5... | collective-permute-start | bytes 786440 | tf_op jit(solution)/shard_map/ppermute | solution.py:21
  160.7 7.6 %collective-permute-start.25 = (bf16[32,4096]{1,0:T(8,128)(2,1)S(1)}, bf16[32,4096]{1,0:T(8,128)(2,1)S(1)}, u32[]{:S(2)}, u32[]{:S(2)}) collective-permute-start(bf16[32,4096]{1,0:T(8,128)(2,1)S(1)} %slice.50), channel_id=1, source_target_pairs={{0,16},{4,20},{8,24},{12,28},{16,0},{20,4},{24,8},{28,12},{1,17},{... | collective-permute-start | bytes 786440 | tf_op jit(solution)/shard_map/ppermute | solution.py:21
  162.1 6.9 %collective-permute-start.28 = (bf16[64,4096]{1,0:T(8,128)(2,1)S(1)}, bf16[64,4096]{1,0:T(8,128)(2,1)S(1)}, u32[]{:S(2)}, u32[]{:S(2)}) collective-permute-start(bf16[64,4096]{1,0:T(8,128)(2,1)S(1)} %collective-permute-done.23), channel_id=1, source_target_pairs={{0,4},{4,0},{8,12},{12,8},{16,20},{20,16},{24,28},{28,24},{1,5},{5... | collective-permute-start | bytes 1572872 | tf_op jit(solution)/shard_map/ppermute | solution.py:21
  162.1 6.8 %collective-permute-start.27 = (bf16[64,4096]{1,0:T(8,128)(2,1)S(1)}, bf16[64,4096]{1,0:T(8,128)(2,1)S(1)}, u32[]{:S(2)}, u32[]{:S(2)}) collective-permute-start(bf16[64,4096]{1,0:T(8,128)(2,1)S(1)} %collective-permute-done.22), channel_id=1, source_target_pairs={{0,4},{4,0},{8,12},{12,8},{16,20},{20,16},{24,28},{28,24},{1,5},{5... | collective-permute-start | bytes 1572872 | tf_op jit(solution)/shard_map/ppermute | solution.py:21
  168.2 1.5 collective-permute-start.29
  168.4 1.8 %collective-permute-start.30 = (bf16[32,4096]{1,0:T(8,128)(2,1)S(1)}, bf16[32,4096]{1,0:T(8,128)(2,1)S(1)}, u32[]{:S(2)}, u32[]{:S(2)}) collective-permute-start(bf16[32,4096]{1,0:T(8,128)(2,1)S(1)} %collective-permute-done.25), channel_id=1, source_target_pairs={{0,4},{4,0},{8,12},{12,8},{16,20},{20,16},{24,28},{28,24},{1,5},{5... | collective-permute-start | bytes 786440 | tf_op jit(solution)/shard_map/ppermute | solution.py:21

commit v2 on v1

v2 whole, which is shorter than its diff:
```python
import functools

import jax
import jax.numpy as jnp
from jax import lax
from jax.experimental import pallas as pl
from jax.experimental.pallas import tpu as pltpu
from jax.sharding import PartitionSpec as P

QH = 32
KVH = 2
HD = 128
NE = 128
TOP = 8
LOG2E = 1.4426950408889634
LOW = -1e30
TILE = 512
STEP = 4
VMEM_MIB = 24


def swap(block, axis, distance):
    count = lax.axis_size(axis)
    return lax.ppermute(block, axis, [(i, i ^ distance) for i in range(count)])


def gather_ctx(block, direct, rider=()):
    count = lax.axis_size("ctx")
    half = block.shape[0] // 2
    far = [(0, 0, block)]
    if direct:
        far += [(d, 0, swap(block, "ctx", d)) for d in range(2, count, 2)]
    elif count == 8:
        along_x, along_y = swap(block, "ctx", 2), swap(block, "ctx", 4)
        far += [(2, 0, along_x), (4, 0, along_y)]
        far += [(6, 0, swap(along_y[:half], "ctx", 2)), (6, half, swap(along_x[half:], "ctx", 4))]
    else:
        distance = 2
        while distance < count:
            far += [(d ^ distance, first, swap(b, "ctx", distance)) for d, first, b in far]
            distance *= 2
    if rider:
        distance, first, last = far[-1]
        last, rider = lax.optimization_barrier((last, rider))
        far[-1] = (distance, first, last)
    return far + [(d ^ 1, first, swap(b, "ctx", 1)) for d, first, b in far], rider


def places_of(named):
    tokens = named.shape[1]
    before = lax.broadcasted_iota(jnp.int32, (tokens, tokens), 0) < lax.broadcasted_iota(
        jnp.int32, (tokens, tokens), 1
    )
    ahead = jnp.dot(
        named.astype(jnp.bfloat16), before.astype(jnp.bfloat16),
        preferred_element_type=jnp.float32,
    )
    index = lax.broadcasted_iota(jnp.int32, (1, tokens), 1).astype(jnp.float32)
    total = jnp.sum(named, axis=1, keepdims=True)
    return jnp.where(named > 0.5, ahead, total + index - ahead).astype(jnp.int32)


def attend_kernel(
    start, tokens, block_len, blocks, order_ref, rank_ref, query_ref, *refs
):
    shards = query_ref.shape[0] // tokens
    masks, pieces, out_ref = refs[:shards], refs[shards:-7], refs[-7]
    key_ref, value_ref, stacked_ref, top_ref, acc_ref, named_ref = refs[-6:]
    for distance in range(shards):
        named_ref[pl.ds(rank_ref[1] ^ distance, 1), :] = masks[distance][...].astype(jnp.float32)
    rows = out_ref.shape[0] // shards
    heads = out_ref.shape[1] // HD
    shards_half = shards // 2
    half_rows = shards_half * rows
    stack = heads * half_rows
    step_len = STEP * block_len

    slot = 0
    for piece in pieces:
        for part in range(piece.shape[0] // block_len):
            distance, at_owner = blocks[slot]
            place = order_ref[2 * (rank_ref[0] ^ distance) + at_owner]
            at = pl.ds(pl.multiple_of(place * block_len, block_len), block_len)
            block = piece[part * block_len:(part + 1) * block_len, :]
            key_ref[at, :HD] = block[:, :HD]
            key_ref[at, HD:] = block[:, :HD]
            value_ref[at, :HD] = block[:, HD:]
            slot += 1
    value_ref[:, HD:] = jnp.ones((value_ref.shape[0], HD), jnp.bfloat16)

    for half in range(2):
        place = order_ref[2 * rank_ref[0] + half]
        offsets = []
        for s in range(shards_half):
            shard = half * shards_half + s
            picked = places_of(named_ref[shard:shard + 1, :]) == start + lax.broadcasted_iota(
                jnp.int32, (rows, tokens), 0
            )
            token = lax.broadcasted_iota(jnp.int32, (rows, tokens), 1)
            offsets.append(
                jnp.sum(jnp.where(picked, token, 0), axis=1, keepdims=True) + s * tokens
            )
            chosen_rows = jnp.dot(
                picked.astype(jnp.bfloat16),
                query_ref[shard * tokens:(shard + 1) * tokens, :],
                preferred_element_type=jnp.float32,
            ) * (LOG2E / HD ** 0.5)
            high = chosen_rows.astype(jnp.bfloat16)
            low = (chosen_rows - high.astype(jnp.float32)).astype(jnp.bfloat16)
            for h in range(heads):
                at = pl.ds(h * half_rows + s * rows, rows)
                stacked_ref[at, :HD] = high[:, h * HD:(h + 1) * HD]
                stacked_ref[at, HD:] = low[:, h * HD:(h + 1) * HD]
        offset = jnp.concatenate(offsets, axis=0)
        query_place = place * block_len + offset
        tile_heads = max(1, min(heads, TILE // half_rows))
        tile = tile_heads * half_rows
        last = place // STEP
        top_ref[...] = jnp.full(top_ref.shape, LOW, jnp.float32)
        acc_ref[...] = jnp.zeros(acc_ref.shape, jnp.float32)

        def absorb(step, masked):
            at = pl.ds(pl.multiple_of(step * step_len, step_len), step_len)
            key_now, value_now = key_ref[at, :], value_ref[at, :]
            if masked:
                key_place = step * step_len + lax.broadcasted_iota(
                    jnp.int32, (half_rows, step_len), 1
                )
                hidden = jnp.where(key_place <= query_place, 0.0, LOW)
                hidden = jnp.concatenate([hidden] * tile_heads, axis=0)

            def score(t):
                scores = lax.dot_general(
                    stacked_ref[t * tile:(t + 1) * tile, :], key_now, (((1,), (1,)), ((), ())),
                    preferred_element_type=jnp.float32,
                )
                return scores + hidden if masked else scores

            ahead = score(0)
            for t in range(stack // tile):
                scores = ahead
                if t + 1 < stack // tile:
                    ahead = score(t + 1)
                here = pl.ds(t * tile, tile)
                top = top_ref[here, :]
                part = scores[:, :HD]
                for c in range(1, step_len // HD):
                    part = jnp.maximum(part, scores[:, c * HD:(c + 1) * HD])
                new_top = jnp.maximum(top, jnp.max(part, axis=1, keepdims=True))
                shrink = jnp.exp2(top - new_top)
                unnormed = jnp.exp2(
                    scores - jnp.concatenate([new_top] * (step_len // HD), axis=1)
                ).astype(jnp.bfloat16)
                added = jnp.dot(unnormed, value_now, preferred_element_type=jnp.float32)
                acc_ref[here, :] = acc_ref[here, :] * jnp.concatenate([shrink] * 2, axis=1) + added
                top_ref[here, :] = new_top

        lax.fori_loop(0, last, lambda step, _: absorb(step, False), None)
        absorb(last, True)
        for h in range(heads):
            here = pl.ds(h * half_rows, half_rows)
            out_ref[half * half_rows:(half + 1) * half_rows, h * HD:(h + 1) * HD] = (
                acc_ref[here, :HD] / acc_ref[here, HD:]
            ).astype(jnp.bfloat16)


def attend(start, rows, queries, named, block_order, rank, blocks, pieces):
    shards, tokens = len(named), named[0].shape[1]
    local_len, width = queries.shape
    block_len = local_len // 2
    seq = len(blocks) * block_len
    stack = width // HD * (shards // 2) * rows
    smem = pl.BlockSpec(memory_space=pltpu.SMEM)
    vmem = pl.BlockSpec(memory_space=pltpu.VMEM)
    return pl.pallas_call(
        functools.partial(attend_kernel, start, tokens, block_len, blocks),
        out_shape=jax.ShapeDtypeStruct((shards * rows, width), jnp.bfloat16),
        in_specs=[smem, smem, vmem] + [vmem] * (shards + len(pieces)),
        out_specs=vmem,
        scratch_shapes=[
            pltpu.VMEM((seq, 2 * HD), jnp.bfloat16),
            pltpu.VMEM((seq, 2 * HD), jnp.bfloat16),
            pltpu.VMEM((stack, 2 * HD), jnp.bfloat16),
            pltpu.VMEM((stack, HD), jnp.float32),
            pltpu.VMEM((stack, 2 * HD), jnp.float32),
            pltpu.VMEM((shards, tokens), jnp.float32),
        ],
        compiler_params=pltpu.CompilerParams(vmem_limit_bytes=VMEM_MIB * 1024 * 1024),
        cost_estimate=pl.CostEstimate(
            flops=4 * stack * 2 * seq * HD, bytes_accessed=6 * 1024 * 1024,
            transcendentals=stack * seq,
        ),
    )(block_order, rank, queries, *named, *pieces)


def finish_kernel(*refs):
    *sums, residual_ref, gain_ref, placing_ref = refs[:7]
    stream_ref, *outgoing = refs[7:]
    half = residual_ref.shape[1] // 2
    square = 0.0
    for c in range(2):
        at = slice(c * half, (c + 1) * half)
        projection = sums[c][...] + sums[2 + c][...].astype(jnp.float32)
        stream = (residual_ref[:, at].astype(jnp.float32) + projection).astype(jnp.bfloat16)
        stream_ref[:, at] = stream
        widened = stream.astype(jnp.float32)
        square = square + jnp.sum(widened * widened, axis=1, keepdims=True)
    scale = lax.rsqrt(square / (2 * half) + 1e-06)
    rows = outgoing[0].shape[0]
    for first in range(0, 2 * half, 512):
        at = slice(first, first + 512)
        normed = (stream_ref[:, at].astype(jnp.float32) * scale * gain_ref[:, at]).astype(
            jnp.bfloat16
        )
        placed = jnp.dot(placing_ref[...], normed, preferred_element_type=jnp.float32)
        for d, out_ref in enumerate(outgoing):
            out_ref[:, at] = placed[d * rows:(d + 1) * rows].astype(jnp.bfloat16)


def finish(keeps, came, residual, gain, placing, places):
    rows, features = residual.shape
    vmem = pl.BlockSpec(memory_space=pltpu.VMEM)
    out = jax.ShapeDtypeStruct((placing.shape[0] // places, features), jnp.bfloat16)
    return pl.pallas_call(
        finish_kernel,
        out_shape=[jax.ShapeDtypeStruct((rows, features), jnp.bfloat16)] + [out] * places,
        in_specs=[vmem] * 7,
        out_specs=[vmem] * (1 + places),
        compiler_params=pltpu.CompilerParams(vmem_limit_bytes=VMEM_MIB * 1024 * 1024),
    )(*keeps, *came, residual, gain, placing)


def scatter_turn(total, column, bit, axis, after=None):
    mine = (column >> bit) & 1
    send = lax.dynamic_index_in_dim(total, 1 - mine, axis, keepdims=False)
    keep = lax.dynamic_index_in_dim(total, mine, axis, keepdims=False)
    came = swap(send.astype(jnp.bfloat16), "exp", 1 << bit)
    if after is not None:
        came, _ = lax.optimization_barrier((came, after))
    return keep, came


def local(queries, keys, values, residual, out_weight, norm_gain, routes, chosen, block_order):
    ctx_count = lax.axis_size("ctx")
    ctx_rank = lax.axis_index("ctx")
    exp_count = lax.axis_size("exp")
    column = lax.axis_index("exp")
    local_len = queries.shape[0]
    block_len = local_len // 2
    seq = ctx_count * local_len
    heads_here = queries.shape[1] // HD
    token_rows, features = residual.shape
    n_chosen = chosen.shape[0]
    per_exp = n_chosen // exp_count
    capacity = 2 * token_rows * TOP // NE

    kv_head = column * heads_here // (QH // KVH)
    key_mine = lax.dynamic_slice_in_dim(keys, kv_head * HD, HD, 1)
    value_mine = lax.dynamic_slice_in_dim(values, kv_head * HD, HD, 1)
    routed = jnp.any(routes[:, :, None] == chosen[None, None, :], axis=1)
    named = jnp.any(routes[:, :, None] == chosen[None, None, :], axis=(1, 2)).astype(jnp.int32)
    named_all = [named[None]] + [swap(named[None], "exp", d) for d in range(1, exp_count)]
    gathered, named_all = gather_ctx(
        jnp.concatenate([key_mine, value_mine], axis=1), True, named_all
    )
    pieces = [piece for _, _, piece in gathered]
    blocks = [
        (distance, first // block_len + part)
        for distance, first, piece in gathered
        for part in range(piece.shape[0] // block_len)
    ]
    rank = jnp.stack([ctx_rank, column]).astype(jnp.int32)

    dest = places_of(named.astype(jnp.float32)[None])
    order = (dest == jnp.arange(token_rows, dtype=jnp.int32)[:, None]).astype(jnp.bfloat16)

    first_rows = min(token_rows, -(-n_chosen * capacity // 16) * 16)
    chunks = [(0, first_rows)]
    if first_rows < token_rows:
        chunks.append((first_rows, token_rows - first_rows))
    bits = exp_count.bit_length() - 1
    residual_ordered = jnp.dot(order, residual, preferred_element_type=jnp.float32).astype(
        jnp.bfloat16
    )
    half = features // 2
    ways = (list(range(bits)), list(range(bits - 1, -1, -1)))

    def attend_chunk(chunk, queries):
        start, rows = chunk
        attention = attend(start, rows, queries, named_all, block_order, rank, blocks, pieces)
        return attention.reshape((2,) * bits + (rows, heads_here * HD))

    def project(attention, columns, stays):
        bit = ways[columns][0]
        index = ((column >> bit) & 1) ^ (not stays)
        picked = lax.dynamic_index_in_dim(attention, index, bits - 1 - bit, keepdims=False)
        return jnp.einsum(
            "...rk,kd->...rd", picked, out_weight[:, columns * half:(columns + 1) * half],
            preferred_element_type=jnp.float32,
        ).astype(jnp.bfloat16)

    def first_turn(sends):
        return [swap(sends[c], "exp", 1 << ways[c][0]) for c in range(2)]

    def add_first(keeps, came):
        totals = [k.astype(jnp.float32) + c.astype(jnp.float32) for k, c in zip(keeps, came)]
        return lax.optimization_barrier(totals)

    def other_turns(totals):
        keeps, cames = [], []
        for c in range(2):
            keep = totals[c]
            live = [bit for bit in range(bits - 1, -1, -1) if bit != ways[c][0]]
            for turn, bit in enumerate(ways[c][1:]):
                if turn > 0:
                    keep = keep.astype(jnp.float32) + came.astype(jnp.float32)
                keep, came = scatter_turn(keep, column, bit, live.index(bit))
                live.remove(bit)
            keeps.append(keep)
            cames.append(came)
        return keeps, cames

    attention = attend_chunk(chunks[0], queries)
    sends = [project(attention, c, False) for c in range(2)]
    came = first_turn(sends)
    keeps = [project(attention, c, True) for c in range(2)]
    if len(chunks) > 1:
        _, queries = lax.optimization_barrier((sends, queries))
        attention_late = attend_chunk(chunks[1], queries)
        came, attention_late = lax.optimization_barrier((came, attention_late))
    keeps, came = other_turns(add_first(keeps, came))

    arrival = jnp.cumsum(routed.astype(jnp.int32), axis=0) - 1
    slot_ids = jnp.arange(capacity, dtype=jnp.int32)
    placing = (routed.T[:, None, :] & (arrival.T[:, None, :] == slot_ids[None, :, None])).astype(
        jnp.bfloat16
    )
    placing = jnp.einsum(
        "est,rt->esr", placing, order[:first_rows], preferred_element_type=jnp.float32
    ).astype(jnp.bfloat16)
    placing = jnp.concatenate(
        [
            lax.dynamic_slice_in_dim(placing, (column ^ d) * per_exp, per_exp, 0)
            for d in range(exp_count)
        ]
    ).reshape(n_chosen * capacity, first_rows)
    stream_first, *outgoing = finish(
        keeps, came, residual_ordered[:first_rows], norm_gain[None], placing, exp_count
    )
    streams = [stream_first]
    arrived = [outgoing[0]] + [swap(outgoing[d], "exp", d) for d in range(1, exp_count)]
    if len(chunks) > 1:
        _, attention_late = lax.optimization_barrier((outgoing, attention_late))
        sends, keeps = [
            [project(attention_late, c, stays) for c in range(2)] for stays in (False, True)
        ]
        arrived, sends = lax.optimization_barrier((arrived, sends))
        came = first_turn(sends)
    rows_mine = jnp.concatenate(arrived, axis=0)
    every = jnp.concatenate([piece for _, _, piece in gather_ctx(rows_mine, False)[0]], axis=0)
    if len(chunks) > 1:
        came, every = lax.optimization_barrier((came, every))
        keeps, came = other_turns(add_first(keeps, came))
        projection = jnp.concatenate(
            [k.astype(jnp.float32) + c.astype(jnp.float32) for k, c in zip(keeps, came)], axis=1
        )
        streams.append((residual_ordered[first_rows:] + projection).astype(jnp.bfloat16))
    stream = jnp.dot(
        order.T, jnp.concatenate(streams, axis=0), preferred_element_type=jnp.float32
    ).astype(jnp.bfloat16)
    rows_dev = features // ctx_count
    own_cols = lax.dynamic_slice_in_dim(every, ctx_rank * rows_dev, rows_dev, 1)
    gram = lax.dot_general(
        own_cols, every, (((0,), (0,)), ((), ())), preferred_element_type=jnp.float32
    )
    mean_rows = seq * TOP // NE
    return (stream, (gram / mean_rows)[None])


def solution(mesh):
    in_specs = (
        P("ctx", "exp"),
        P("ctx", None),
        P("ctx", None),
        P(("ctx", "exp"), None),
        P("exp", None),
        P(),
        P(("ctx", "exp"), None),
        P(),
        P(),
    )
    out_specs = (P(("ctx", "exp"), None), P("exp", "ctx", None))
    return jax.shard_map(local, mesh=mesh, in_specs=in_specs, out_specs=out_specs, check_vma=False)
```

time: 176 us -> 149 us (0.85)
  waiting for transfers between devices: 81 us -> 59.2 us
  Pallas kernels: 44.2 us -> 25.4 us
  matrix products: 15.3 us -> 21.9 us
  local copies, waits for them, and re-layouts: 3.51 us -> 9.77 us
  starting transfers between devices: 23.7 us -> 29 us
  other arithmetic: 6.89 us -> 2.26 us
    ppermute x31 -> x30, waiting for transfers between devices: 81 us -> 59.2 us  [swap(): return lax.ppermute(block, axis, [(i, i ^ distance) for i in range(count)])]
    pallas_call x2 -> x3, Pallas kernels: 44.2 us -> 25.4 us  [the longest x2 24.8 us: attend(): pl.pallas_call(functools.partial(attend_kernel, start, tokens, block_len,...]
    dot_general x9 -> x10, matrix products: 6.27 us -> 13.2 us  [the longest x8 12.3 us: project(): jnp.einsum('...rk,kd->...rd', picked, out_weight[:, columns * half:(colum...]
    unnamed x46 -> x55, local copies, waits for them, and re-layouts: 0.37 us -> 7.22 us
    ppermute x31 -> x30, starting transfers between devices: 23.7 us -> 29 us  [swap(): return lax.ppermute(block, axis, [(i, i ^ distance) for i in range(count)])]
    select_n x5 -> x0, other arithmetic: 2.85 us -> none  [the longest x2 1.3 us: local(): jnp.where(named == 1, jnp.cumsum(named) - 1, jnp.sum(named) + jnp.cumsum(...]
  transfers between devices with their start and end apart: 31 -> 30, of which waited for: 17 -> 18; matrix products, arithmetic and copies ran while one was open for 9% -> 11% of each run, Pallas kernels for 0% -> 8%
where the time goes in v2:
time: 149 us
  waiting for transfers between devices  59.2 us (40%)
  starting transfers between devices  29 us (19%)
  Pallas kernels  25.4 us (17%)
  matrix products  21.9 us (15%)
  local copies, waits for them, and re-layouts  9.77 us (7%)
  other arithmetic  2.26 us (2%)
    ppermute x30, waiting for transfers between devices, swap(): return lax.ppermute(block, axis, [(i, i ^ distance) for i in range(count)])  59.2 us
    ppermute x30, starting transfers between devices, swap(): return lax.ppermute(block, axis, [(i, i ^ distance) for i in range(count)])  29 us
    pallas_call x2, Pallas kernels, attend(): pl.pallas_call(functools.partial(attend_kernel, start, tokens, block_len,...  24.8 us
    dot_general x8, matrix products, project(): jnp.einsum('...rk,kd->...rd', picked, out_weight[:, columns * half:(colum...  12.3 us
    unnamed x55, local copies, waits for them, and re-layouts  7.22 us
    dot_general x1, matrix products, local(): lax.dot_general(own_cols, every, (((0,), (0,)), ((), ())), preferred_elem...  5.82 us
  transfers between devices with their start and end apart: 30, of which 18 were waited for; matrix products, arithmetic and copies ran while one was open for 11% of the time, Pallas kernels for 8%

profile of v2, /device:TPU:0, one launch (start us, length us, event | category | flops | bytes accessed | tf_op | source)
XLA Modules:
  0.0 148.7 jit_solution(8354926408814069906)
XLA Ops:
  0.6 0.9 compare_reduce_fusion
  1.5 3.1 %collective-permute-start.1 = (s32[1,128]{1,0:T(1,128)S(1)}, s32[1,128]{1,0:T(1,128)S(1)}, u32[]{:S(2)}, u32[]{:S(2)}) collective-permute-start(s32[1,128]{1,0:T(1,128)S(1)} %convert_bitcast_fusion.refs_0_), channel_id=1, source_target_pairs={{0,1},{1,0},{2,3},{3,2},{4,5},{5,4},{6,7},{7,6},{8,9},{9,8},{10,11... | collective-permute-start | bytes 1544 | tf_op jit(solution)/shard_map/ppermute | solution.py:24
  4.6 2.6 %collective-permute-start.2 = (s32[1,128]{1,0:T(1,128)S(1)}, s32[1,128]{1,0:T(1,128)S(1)}, u32[]{:S(2)}, u32[]{:S(2)}) collective-permute-start(s32[1,128]{1,0:T(1,128)S(1)} %convert_bitcast_fusion.refs_0_), channel_id=1, source_target_pairs={{0,2},{1,3},{2,0},{3,1},{4,6},{5,7},{6,4},{7,5},{8,10},{9,11},{10,... | collective-permute-start | bytes 1544 | tf_op jit(solution)/shard_map/ppermute | solution.py:24
  7.2 1.0 constant_dynamic-slice_fusion.4
  8.2 2.5 %collective-permute-start = (bf16[512,256]{1,0:T(8,128)(2,1)S(1)}, bf16[512,256]{1,0:T(8,128)(2,1)S(1)}, u32[]{:S(2)}, u32[]{:S(2)}) collective-permute-start(bf16[512,256]{1,0:T(8,128)(2,1)S(1)} %pad_maximum_fusion.refs_4_), channel_id=1, source_target_pairs={{0,24},{4,28},{8,16},{12,20},{16,8},{20,12},{24,0},{28,4},{1,25},{... | collective-permute-start | bytes 786440 | tf_op jit(solution)/shard_map/ppermute | solution.py:24
  10.7 0.5 collective-permute-start.4
  11.3 0.5 collective-permute-start.5
  11.8 0.6 convert_reduce_fusion
  12.4 0.8 fusion.106
  13.3 0.2 reduce_window_sum.11
  13.9 5.2 %collective-permute-done.3.refs_3_ = s32[1,128]{1,0:T(1,128)S(1)} collective-permute-done((s32[1,128]{1,0:T(1,128)S(1)}, s32[1,128]{1,0:T(1,128)S(1)}, u32[]{:S(2)}, u32[]{:S(2)}) %collective-permute-start.3) | collective-permute-done | bytes 544 | tf_op jit(solution)/shard_map/ppermute | solution.py:24
  19.1 3.2 %collective-permute-done.4.refs_5_ = bf16[512,256]{1,0:T(8,128)(2,1)S(1)} collective-permute-done((bf16[512,256]{1,0:T(8,128)(2,1)S(1)}, bf16[512,256]{1,0:T(8,128)(2,1)S(1)}, u32[]{:S(2)}, u32[]{:S(2)}) %collective-permute-start.4) | collective-permute-done | bytes 262176 | tf_op jit(solution)/shard_map/ppermute | solution.py:24
  22.4 0.5 collective-permute-start.8
  22.9 1.4 convolution_convert_fusion.1
  24.4 1.5 copy-done.2
  25.9 0.7 copy-done.14
  26.5 12.3 %shard_map.104 = bf16[256,1024]{1,0:T(8,128)(2,1)S(1)} custom-call(s32[16]{0:T(128)S(1)} %copy-done.14, s32[2]{0:T(128)S(1)} %pad_add_fusion.rank_ref, bf16[512,1024]{1,0:T(8,128)(2,1)S(1)} %copy-done.2, s32[1,128]{1,0:T(1,128)S(1)} %convert_bitcast_fusion.refs_0_, s32[1,128]{1,0:T(1,128)S(1)} %collective-permute-done.1.refs_1_, ...), custom_call_target="tpu_custom_call" | custom-call | flops 4294967296 | bytes 6291456 | tf_op jit(solution)/shard_map/pallas_call | solution.py:175
  38.9 1.5 %fusion.33 = bf16[2,64,2048]{2,1,0:T(8,128)(2,1)} fusion(bf16[1024,4096]{1,0:T(8,128)(2,1)S(1)} %copy-done.19, bf16[2,2,64,1024]{3,2,1,0:T(8,128)(2,1)S(1)} %bitcast.119, s32[]{:T(128)S(6)} %select_n.64), kind=kOutput, calls=%fused_computation.30 | convolution fusion | flops 537133056 | bytes 4980740 | tf_op jit(solution)/shard_map/...rk,kd->...rd/dot_general | solution.py:297
  40.5 0.5 collective-permute-start.10
  40.9 1.5 %fusion.45 = bf16[2,64,2048]{2,1,0:T(8,128)(2,1)} fusion(bf16[1024,4096]{1,0:T(8,128)(2,1)S(1)} %copy-done.19, bf16[2,2,64,1024]{3,2,1,0:T(8,128)(2,1)S(1)} %bitcast.120, s32[]{:T(128)S(6)} %select_n.65), kind=kOutput, calls=%fused_computation.34 | convolution fusion | flops 537133056 | bytes 4980740 | tf_op jit(solution)/shard_map/...rk,kd->...rd/dot_general | solution.py:297
  42.4 0.3 collective-permute-start.11
  42.8 1.1 slice.34.refs_4_
  43.9 0.9 copy-done.5
  44.8 0.9 copy-done.7
  45.8 0.9 copy-done.9
  46.7 0.9 copy-done.11
  47.7 0.9 copy-done.13
  48.6 12.5 %shard_map.105 = bf16[256,1024]{1,0:T(8,128)(2,1)S(1)} custom-call(s32[16]{0:T(128)S(1)} %copy-done.15, s32[2]{0:T(128)S(1)} %pad_add_fusion.rank_ref, bf16[512,1024]{1,0:T(8,128)(2,1)S(1)} %copy-done.3, s32[1,128]{1,0:T(1,128)S(1)} %convert_bitcast_fusion.refs_0_, s32[1,128]{1,0:T(1,128)S(1)} %collective-permute-done.1.refs_1_, ...), custom_call_target="tpu_custom_call" | custom-call | flops 4294967296 | bytes 6291456 | tf_op jit(solution)/shard_map/pallas_call | solution.py:175
  61.2 0.6 collective-permute-done.10
  61.7 5.4 %collective-permute-done.11 = bf16[2,64,2048]{2,1,0:T(8,128)(2,1)} collective-permute-done((bf16[2,64,2048]{2,1,0:T(8,128)(2,1)}, bf16[2,64,2048]{2,1,0:T(8,128)(2,1)}, u32[]{:S(2)}, u32[]{:S(2)}) %collective-permute-start.11) | collective-permute-done | bytes 524320 | tf_op jit(solution)/shard_map/ppermute | solution.py:24
  67.1 3.2 %fusion.30 = f32[2,64,2048]{2,1,0:T(8,128)S(1)} fusion(bf16[1024,4096]{1,0:T(8,128)(2,1)} %param.13, bf16[2,64,2048]{2,1,0:T(8,128)(2,1)} %collective-permute-done.10, bf16[2,2,64,1024]{3,2,1,0:T(8,128)(2,1)S(1)} %bitcast.121, s32[]{:T(128)S(6)} %select_n.63), kind=kOutput, calls=%fused_computation.29 | convolution fusion | flops 537919488 | bytes 6029316 | tf_op jit(solution)/shard_map/...rk,kd->...rd/dot_general | solution.py:297
  70.3 3.2 %fusion.54 = f32[2,64,2048]{2,1,0:T(8,128)S(1)} fusion(bf16[1024,4096]{1,0:T(8,128)(2,1)} %param.13, bf16[2,64,2048]{2,1,0:T(8,128)(2,1)} %collective-permute-done.11, bf16[2,2,64,1024]{3,2,1,0:T(8,128)(2,1)S(1)} %bitcast.122, s32[]{:T(128)S(6)} %select_n.66), kind=kOutput, calls=%fused_computation.37 | convolution fusion | flops 537919488 | bytes 6029316 | tf_op jit(solution)/shard_map/...rk,kd->...rd/dot_general | solution.py:297
  73.7 2.0 %collective-permute-start.13 = (bf16[64,2048]{1,0:T(8,128)(2,1)S(1)}, bf16[64,2048]{1,0:T(8,128)(2,1)S(1)}, u32[]{:S(2)}, u32[]{:S(2)}) collective-permute-start(bf16[64,2048]{1,0:T(8,128)(2,1)S(1)} %fusion.72), channel_id=1, source_target_pairs={{0,1},{1,0},{2,3},{3,2},{4,5},{5,4},{6,7},{7,6},{8,9},{9,8},{10,11... | collective-permute-start | bytes 786440 | tf_op jit(solution)/shard_map/ppermute | solution.py:24
  75.8 7.7 %collective-permute-done.12.refs_2_ = bf16[64,2048]{1,0:T(8,128)(2,1)S(1)} collective-permute-done((bf16[64,2048]{1,0:T(8,128)(2,1)S(1)}, bf16[64,2048]{1,0:T(8,128)(2,1)S(1)}, u32[]{:S(2)}, u32[]{:S(2)}) %collective-permute-start.12) | collective-permute-done | bytes 262176 | tf_op jit(solution)/shard_map/ppermute | solution.py:24
  83.4 1.7 %collective-permute-done.13.refs_3_ = bf16[64,2048]{1,0:T(8,128)(2,1)S(1)} collective-permute-done((bf16[64,2048]{1,0:T(8,128)(2,1)S(1)}, bf16[64,2048]{1,0:T(8,128)(2,1)S(1)}, u32[]{:S(2)}, u32[]{:S(2)}) %collective-permute-start.13) | collective-permute-done | bytes 262176 | tf_op jit(solution)/shard_map/ppermute | solution.py:24
  85.1 0.6 shard_map.106
  85.6 0.2 collective-permute-start.14
  85.9 0.7 collective-permute-start.15
  86.6 3.5 %collective-permute-start.16 = (bf16[16,4096]{1,0:T(8,128)(2,1)S(1)}, bf16[16,4096]{1,0:T(8,128)(2,1)S(1)}, u32[]{:S(2)}, u32[]{:S(2)}) collective-permute-start(bf16[16,4096]{1,0:T(8,128)(2,1)S(1)} %get-tuple-element.44), channel_id=1, source_target_pairs={{0,3},{1,2},{2,1},{3,0},{4,7},{5,6},{6,5},{7,4},{8,11},{9,10},{10,... | collective-permute-start | bytes 393224 | tf_op jit(solution)/shard_map/ppermute | solution.py:24
  90.1 0.7 fusion.42
  90.8 0.7 fusion.57
  91.6 6.1 %collective-permute-done.15 = bf16[16,4096]{1,0:T(8,128)(2,1)S(1)} collective-permute-done((bf16[16,4096]{1,0:T(8,128)(2,1)S(1)}, bf16[16,4096]{1,0:T(8,128)(2,1)S(1)}, u32[]{:S(2)}, u32[]{:S(2)}) %collective-permute-start.15) | collective-permute-done | bytes 131104 | tf_op jit(solution)/shard_map/ppermute | solution.py:24
  97.8 1.9 %collective-permute-start.19 = (bf16[64,4096]{1,0:T(8,128)(2,1)S(1)}, bf16[64,4096]{1,0:T(8,128)(2,1)S(1)}, u32[]{:S(2)}, u32[]{:S(2)}) collective-permute-start(bf16[64,4096]{1,0:T(8,128)(2,1)S(1)} %get-tuple-element.60), channel_id=1, source_target_pairs={{0,8},{4,12},{8,0},{12,4},{16,24},{20,28},{24,16},{28,20},{1,9},{5... | collective-permute-start | bytes 1572872 | tf_op jit(solution)/shard_map/ppermute | solution.py:24
  99.7 1.8 %collective-permute-start.20 = (bf16[64,4096]{1,0:T(8,128)(2,1)S(1)}, bf16[64,4096]{1,0:T(8,128)(2,1)S(1)}, u32[]{:S(2)}, u32[]{:S(2)}) collective-permute-start(bf16[64,4096]{1,0:T(8,128)(2,1)S(1)} %get-tuple-element.60), channel_id=1, source_target_pairs={{0,16},{4,20},{8,24},{12,28},{16,0},{20,4},{24,8},{28,12},{1,17},{... | collective-permute-start | bytes 1572872 | tf_op jit(solution)/shard_map/ppermute | solution.py:24
  101.5 0.7 fusion.39
  102.2 0.7 fusion.63
  103.0 3.2 %collective-permute-start.17 = (bf16[2,64,2048]{2,1,0:T(8,128)(2,1)S(1)}, bf16[2,64,2048]{2,1,0:T(8,128)(2,1)S(1)}, u32[]{:S(2)}, u32[]{:S(2)}) collective-permute-start(bf16[2,64,2048]{2,1,0:T(8,128)(2,1)S(1)} %fusion.42), channel_id=1, source_target_pairs={{0,1},{1,0},{2,3},{3,2},{4,5},{5,4},{6,7},{7,6},{8,9},{9,8},{10,11... | collective-permute-start | bytes 1572872 | tf_op jit(solution)/shard_map/ppermute | solution.py:24
  106.3 6.7 %collective-permute-done.20 = bf16[64,4096]{1,0:T(8,128)(2,1)S(1)} collective-permute-done((bf16[64,4096]{1,0:T(8,128)(2,1)S(1)}, bf16[64,4096]{1,0:T(8,128)(2,1)S(1)}, u32[]{:S(2)}, u32[]{:S(2)}) %collective-permute-start.20) | collective-permute-done | bytes 524320 | tf_op jit(solution)/shard_map/ppermute | solution.py:24
  113.0 0.4 collective-permute-start.21
  113.5 1.8 %collective-permute-start.22 = (bf16[32,4096]{1,0:T(8,128)(2,1)S(1)}, bf16[32,4096]{1,0:T(8,128)(2,1)S(1)}, u32[]{:S(2)}, u32[]{:S(2)}) collective-permute-start(bf16[32,4096]{1,0:T(8,128)(2,1)S(1)} %slice.38), channel_id=1, source_target_pairs={{0,16},{4,20},{8,24},{12,28},{16,0},{20,4},{24,8},{28,12},{1,17},{... | collective-permute-start | bytes 786440 | tf_op jit(solution)/shard_map/ppermute | solution.py:24
  115.4 4.4 %collective-permute-done.21 = bf16[32,4096]{1,0:T(8,128)(2,1)S(1)} collective-permute-done((bf16[32,4096]{1,0:T(8,128)(2,1)S(1)}, bf16[32,4096]{1,0:T(8,128)(2,1)S(1)}, u32[]{:S(2)}, u32[]{:S(2)}) %collective-permute-start.21) | collective-permute-done | bytes 262176 | tf_op jit(solution)/shard_map/ppermute | solution.py:24
  119.8 0.4 collective-permute-done.22
  120.5 0.4 collective-permute-start.26
  120.9 0.8 collective-permute-done.24
  121.9 0.6 collective-permute-done.25
  122.5 0.3 collective-permute-done.26
  122.9 0.4 collective-permute-done.27
  123.3 5.5 %collective-permute-done.17 = bf16[2,64,2048]{2,1,0:T(8,128)(2,1)S(1)} collective-permute-done((bf16[2,64,2048]{2,1,0:T(8,128)(2,1)S(1)}, bf16[2,64,2048]{2,1,0:T(8,128)(2,1)S(1)}, u32[]{:S(2)}, u32[]{:S(2)}) %collective-permute-start.17) | collective-permute-done | bytes 524320 | tf_op jit(solution)/shard_map/ppermute | solution.py:24
  128.8 3.7 %collective-permute-done.18 = bf16[2,64,2048]{2,1,0:T(8,128)(2,1)S(1)} collective-permute-done((bf16[2,64,2048]{2,1,0:T(8,128)(2,1)S(1)}, bf16[2,64,2048]{2,1,0:T(8,128)(2,1)S(1)}, u32[]{:S(2)}, u32[]{:S(2)}) %collective-permute-start.18) | collective-permute-done | bytes 524320 | tf_op jit(solution)/shard_map/ppermute | solution.py:24
  132.9 1.9 %collective-permute-start.28 = (bf16[64,2048]{1,0:T(8,128)(2,1)S(1)}, bf16[64,2048]{1,0:T(8,128)(2,1)S(1)}, u32[]{:S(2)}, u32[]{:S(2)}) collective-permute-start(bf16[64,2048]{1,0:T(8,128)(2,1)S(1)} %fusion.73), channel_id=1, source_target_pairs={{0,2},{1,3},{2,0},{3,1},{4,6},{5,7},{6,4},{7,5},{8,10},{9,11},{10,... | collective-permute-start | bytes 786440 | tf_op jit(solution)/shard_map/ppermute | solution.py:24
  134.8 5.8 %multiply_bitcast_fusion = f32[1,512,4096]{2,1,0:T(8,128)} fusion(bf16[512,4096]{1,0:T(8,128)(2,1)S(1)} %constant_dynamic-update-slice_fusion.4, s32[]{:T(128)S(6)} %select_n.73), kind=kOutput, calls=%fused_computation | convolution fusion | flops 2149580800 | bytes 13107204 | tf_op jit(solution)/shard_map/dot_general | solution.py:373
  140.6 4.4 %collective-permute-done.29 = bf16[64,2048]{1,0:T(8,128)(2,1)S(1)} collective-permute-done((bf16[64,2048]{1,0:T(8,128)(2,1)S(1)}, bf16[64,2048]{1,0:T(8,128)(2,1)S(1)}, u32[]{:S(2)}, u32[]{:S(2)}) %collective-permute-start.29) | collective-permute-done | bytes 262176 | tf_op jit(solution)/shard_map/ppermute | solution.py:24
  145.1 2.0 %collective-permute-done.28 = bf16[64,2048]{1,0:T(8,128)(2,1)S(1)} collective-permute-done((bf16[64,2048]{1,0:T(8,128)(2,1)S(1)}, bf16[64,2048]{1,0:T(8,128)(2,1)S(1)}, u32[]{:S(2)}, u32[]{:S(2)}) %collective-permute-start.28) | collective-permute-done | bytes 262176 | tf_op jit(solution)/shard_map/ppermute | solution.py:24
  147.3 1.5 convolution_convert_fusion
  (98 shorter events, 2.3 us)
Async XLA Ops:
  0.6 22.3 %copy-start = (bf16[128,4096]{1,0:T(8,128)(2,1)S(1)}, bf16[128,4096]{1,0:T(8,128)(2,1)}, u32[]{:S(2)}) copy-start(bf16[128,4096]{1,0:T(8,128)(2,1)} %param.12) | copy-start | bytes 3145732
  1.5 12.3 %collective-permute-start.1 = (s32[1,128]{1,0:T(1,128)S(1)}, s32[1,128]{1,0:T(1,128)S(1)}, u32[]{:S(2)}, u32[]{:S(2)}) collective-permute-start(s32[1,128]{1,0:T(1,128)S(1)} %convert_bitcast_fusion.refs_0_), channel_id=1, source_target_pairs={{0,1},{1,0},{2,3},{3,2},{4,5},{5,4},{6,7},{7,6},{8,9},{9,8},{10,11... | collective-permute-start | bytes 1544 | tf_op jit(solution)/shard_map/ppermute | solution.py:24
  4.6 9.2 %collective-permute-start.2 = (s32[1,128]{1,0:T(1,128)S(1)}, s32[1,128]{1,0:T(1,128)S(1)}, u32[]{:S(2)}, u32[]{:S(2)}) collective-permute-start(s32[1,128]{1,0:T(1,128)S(1)} %convert_bitcast_fusion.refs_0_), channel_id=1, source_target_pairs={{0,2},{1,3},{2,0},{3,1},{4,6},{5,7},{6,4},{7,5},{8,10},{9,11},{10,... | collective-permute-start | bytes 1544 | tf_op jit(solution)/shard_map/ppermute | solution.py:24
  8.2 10.9 %collective-permute-start = (bf16[512,256]{1,0:T(8,128)(2,1)S(1)}, bf16[512,256]{1,0:T(8,128)(2,1)S(1)}, u32[]{:S(2)}, u32[]{:S(2)}) collective-permute-start(bf16[512,256]{1,0:T(8,128)(2,1)S(1)} %pad_maximum_fusion.refs_4_), channel_id=1, source_target_pairs={{0,24},{4,28},{8,16},{12,20},{16,8},{20,12},{24,0},{28,4},{1,25},{... | collective-permute-start | bytes 786440 | tf_op jit(solution)/shard_map/ppermute | solution.py:24
  10.7 11.7 %collective-permute-start.4 = (bf16[512,256]{1,0:T(8,128)(2,1)S(1)}, bf16[512,256]{1,0:T(8,128)(2,1)S(1)}, u32[]{:S(2)}, u32[]{:S(2)}) collective-permute-start(bf16[512,256]{1,0:T(8,128)(2,1)S(1)} %pad_maximum_fusion.refs_4_), channel_id=1, source_target_pairs={{0,8},{4,12},{8,0},{12,4},{16,24},{20,28},{24,16},{28,20},{1,9},{5... | collective-permute-start | bytes 786440 | tf_op jit(solution)/shard_map/ppermute | solution.py:24
  11.3 11.1 %collective-permute-start.5 = (bf16[512,256]{1,0:T(8,128)(2,1)S(1)}, bf16[512,256]{1,0:T(8,128)(2,1)S(1)}, u32[]{:S(2)}, u32[]{:S(2)}) collective-permute-start(bf16[512,256]{1,0:T(8,128)(2,1)S(1)} %pad_maximum_fusion.refs_4_), channel_id=1, source_target_pairs={{0,16},{4,20},{8,24},{12,28},{16,0},{20,4},{24,8},{28,12},{1,17},{... | collective-permute-start | bytes 786440 | tf_op jit(solution)/shard_map/ppermute | solution.py:24
  13.8 5.4 %collective-permute-start.3 = (s32[1,128]{1,0:T(1,128)S(1)}, s32[1,128]{1,0:T(1,128)S(1)}, u32[]{:S(2)}, u32[]{:S(2)}) collective-permute-start(s32[1,128]{1,0:T(1,128)S(1)} %convert_bitcast_fusion.refs_0_), channel_id=1, source_target_pairs={{0,3},{1,2},{2,1},{3,0},{4,7},{5,6},{6,5},{7,4},{8,11},{9,10},{10,... | collective-permute-start | bytes 1544 | tf_op jit(solution)/shard_map/ppermute | solution.py:24
  13.8 10.5 %collective-permute-start.6 = (bf16[512,256]{1,0:T(8,128)(2,1)S(1)}, bf16[512,256]{1,0:T(8,128)(2,1)S(1)}, u32[]{:S(2)}, u32[]{:S(2)}) collective-permute-start(bf16[512,256]{1,0:T(8,128)(2,1)S(1)} %pad_maximum_fusion.refs_4_), channel_id=1, source_target_pairs={{0,4},{4,0},{8,12},{12,8},{16,20},{20,16},{24,28},{28,24},{1,5},{5... | collective-permute-start | bytes 786440 | tf_op jit(solution)/shard_map/ppermute | solution.py:24
  19.1 5.2 %collective-permute-start.9 = (bf16[512,256]{1,0:T(8,128)(2,1)S(1)}, bf16[512,256]{1,0:T(8,128)(2,1)S(1)}, u32[]{:S(2)}, u32[]{:S(2)}) collective-permute-start(bf16[512,256]{1,0:T(8,128)(2,1)S(1)} %collective-permute-done.refs_7_), channel_id=1, source_target_pairs={{0,4},{4,0},{8,12},{12,8},{16,20},{20,16},{24,28},{28,24},{1,5},{5... | collective-permute-start | bytes 786440 | tf_op jit(solution)/shard_map/ppermute | solution.py:24
  22.4 1.9 %collective-permute-start.7 = (bf16[512,256]{1,0:T(8,128)(2,1)S(1)}, bf16[512,256]{1,0:T(8,128)(2,1)S(1)}, u32[]{:S(2)}, u32[]{:S(2)}) collective-permute-start(bf16[512,256]{1,0:T(8,128)(2,1)S(1)} %collective-permute-done.4.refs_5_), channel_id=1, source_target_pairs={{0,4},{4,0},{8,12},{12,8},{16,20},{20,16},{24,28},{28,24},{1,5},{5... | collective-permute-start | bytes 786440 | tf_op jit(solution)/shard_map/ppermute | solution.py:24
  22.4 16.5 %copy-start.4 = (bf16[512,256]{1,0:T(8,128)(2,1)}, bf16[512,256]{1,0:T(8,128)(2,1)S(1)}, u32[]{:S(2)}) copy-start(bf16[512,256]{1,0:T(8,128)(2,1)S(1)} %collective-permute-done.5.refs_6_) | copy-start | bytes 786436
  22.4 1.9 %collective-permute-start.8 = (bf16[512,256]{1,0:T(8,128)(2,1)S(1)}, bf16[512,256]{1,0:T(8,128)(2,1)S(1)}, u32[]{:S(2)}, u32[]{:S(2)}) collective-permute-start(bf16[512,256]{1,0:T(8,128)(2,1)S(1)} %collective-permute-done.5.refs_6_), channel_id=1, source_target_pairs={{0,4},{4,0},{8,12},{12,8},{16,20},{20,16},{24,28},{28,24},{1,5},{5... | collective-permute-start | bytes 786440 | tf_op jit(solution)/shard_map/ppermute | solution.py:24
  24.3 14.5 %copy-start.6 = (bf16[512,256]{1,0:T(8,128)(2,1)}, bf16[512,256]{1,0:T(8,128)(2,1)S(1)}, u32[]{:S(2)}) copy-start(bf16[512,256]{1,0:T(8,128)(2,1)S(1)} %collective-permute-done.6.refs_8_) | copy-start | bytes 786436
  24.3 14.5 %copy-start.10 = (bf16[512,256]{1,0:T(8,128)(2,1)}, bf16[512,256]{1,0:T(8,128)(2,1)S(1)}, u32[]{:S(2)}) copy-start(bf16[512,256]{1,0:T(8,128)(2,1)S(1)} %collective-permute-done.7.refs_9_) | copy-start | bytes 786436
  24.3 14.5 %copy-start.12 = (bf16[512,256]{1,0:T(8,128)(2,1)}, bf16[512,256]{1,0:T(8,128)(2,1)S(1)}, u32[]{:S(2)}) copy-start(bf16[512,256]{1,0:T(8,128)(2,1)S(1)} %collective-permute-done.8.refs_10_) | copy-start | bytes 786436
  24.4 1.5 copy-start.2
  25.8 0.7 copy-start.14
  26.5 12.4 %copy-start.8 = (bf16[512,256]{1,0:T(8,128)(2,1)}, bf16[512,256]{1,0:T(8,128)(2,1)S(1)}, u32[]{:S(2)}) copy-start(bf16[512,256]{1,0:T(8,128)(2,1)S(1)} %collective-permute-done.9.refs_11_) | copy-start | bytes 786436
  26.5 12.4 %copy-start.19 = (bf16[1024,4096]{1,0:T(8,128)(2,1)S(1)}, bf16[1024,4096]{1,0:T(8,128)(2,1)}, u32[]{:S(2)}) copy-start(bf16[1024,4096]{1,0:T(8,128)(2,1)} %param.13) | copy-start | bytes 25165828
  38.9 2.0 %copy-start.16 = (bf16[256,1024]{1,0:T(8,128)(2,1)}, bf16[256,1024]{1,0:T(8,128)(2,1)S(1)}, u32[]{:S(2)}) copy-start(bf16[256,1024]{1,0:T(8,128)(2,1)S(1)} %shard_map.104) | copy-start | bytes 1572868
  40.5 3.4 %copy-start.3 = (bf16[512,1024]{1,0:T(8,128)(2,1)S(1)}, bf16[512,1024]{1,0:T(8,128)(2,1)}, u32[]{:S(2)}) copy-start(bf16[512,1024]{1,0:T(8,128)(2,1)} %query_ref.2) | copy-start | bytes 3145732
  40.5 3.4 %copy-start.15 = (s32[16]{0:T(128)S(1)}, s32[16]{0:T(128)}, u32[]{:S(2)}) copy-start(s32[16]{0:T(128)} %order_ref.3) | copy-start | bytes 196
  40.5 21.3 %collective-permute-start.10 = (bf16[2,64,2048]{2,1,0:T(8,128)(2,1)}, bf16[2,64,2048]{2,1,0:T(8,128)(2,1)}, u32[]{:S(2)}, u32[]{:S(2)}) collective-permute-start(bf16[2,64,2048]{2,1,0:T(8,128)(2,1)} %fusion.33), channel_id=1, source_target_pairs={{0,1},{1,0},{2,3},{3,2},{4,5},{5,4},{6,7},{7,6},{8,9},{9,8},{10,11... | collective-permute-start | bytes 1572872 | tf_op jit(solution)/shard_map/ppermute | solution.py:24
  42.4 24.7 %collective-permute-start.11 = (bf16[2,64,2048]{2,1,0:T(8,128)(2,1)}, bf16[2,64,2048]{2,1,0:T(8,128)(2,1)}, u32[]{:S(2)}, u32[]{:S(2)}) collective-permute-start(bf16[2,64,2048]{2,1,0:T(8,128)(2,1)} %fusion.45), channel_id=1, source_target_pairs={{0,2},{1,3},{2,0},{3,1},{4,6},{5,7},{6,4},{7,5},{8,10},{9,11},{10,... | collective-permute-start | bytes 1572872 | tf_op jit(solution)/shard_map/ppermute | solution.py:24
  43.9 1.0 copy-start.5
  44.8 0.9 copy-start.7
  45.8 0.9 copy-start.9
  46.7 0.9 copy-start.11
  47.7 0.9 copy-start.13
  48.6 18.5 %copy-start.17 = (bf16[256,1024]{1,0:T(8,128)(2,1)S(1)}, bf16[256,1024]{1,0:T(8,128)(2,1)}, u32[]{:S(2)}) copy-start(bf16[256,1024]{1,0:T(8,128)(2,1)} %copy-done.16) | copy-start | bytes 1572868
  67.1 23.0 %slice-start = ((s8[8388608]{0:T(1024)(128)(4,1)}), s8[4194304]{0:T(1024)(128)(4,1)S(1)}, s32[]{:S(2)}) async-start(s8[8388608]{0:T(1024)(128)(4,1)} %bitcast.124), calls=%async_computation | async-start | bytes 8388608
  70.3 14.8 %copy-start.1 = (f32[4096]{0:T(1024)S(1)}, f32[4096]{0:T(1024)}, u32[]{:S(2)}) copy-start(f32[4096]{0:T(1024)} %param.14) | copy-start | bytes 49156
  70.3 19.8 %slice-start.1 = ((s8[8388608]{0:T(1024)(128)(4,1)}), s8[4194304]{0:T(1024)(128)(4,1)S(1)}, s32[]{:S(2)}) async-start(s8[8388608]{0:T(1024)(128)(4,1)} %bitcast.124), calls=%async_computation.1 | async-start | bytes 8388608
  73.6 9.8 %collective-permute-start.12 = (bf16[64,2048]{1,0:T(8,128)(2,1)S(1)}, bf16[64,2048]{1,0:T(8,128)(2,1)S(1)}, u32[]{:S(2)}, u32[]{:S(2)}) collective-permute-start(bf16[64,2048]{1,0:T(8,128)(2,1)S(1)} %fusion.71), channel_id=1, source_target_pairs={{0,2},{1,3},{2,0},{3,1},{4,6},{5,7},{6,4},{7,5},{8,10},{9,11},{10,... | collective-permute-start | bytes 786440 | tf_op jit(solution)/shard_map/ppermute | solution.py:24
  73.7 11.4 %collective-permute-start.13 = (bf16[64,2048]{1,0:T(8,128)(2,1)S(1)}, bf16[64,2048]{1,0:T(8,128)(2,1)S(1)}, u32[]{:S(2)}, u32[]{:S(2)}) collective-permute-start(bf16[64,2048]{1,0:T(8,128)(2,1)S(1)} %fusion.72), channel_id=1, source_target_pairs={{0,1},{1,0},{2,3},{3,2},{4,5},{5,4},{6,7},{7,6},{8,9},{9,8},{10,11... | collective-permute-start | bytes 786440 | tf_op jit(solution)/shard_map/ppermute | solution.py:24
  85.6 5.9 %collective-permute-start.14 = (bf16[16,4096]{1,0:T(8,128)(2,1)S(1)}, bf16[16,4096]{1,0:T(8,128)(2,1)S(1)}, u32[]{:S(2)}, u32[]{:S(2)}) collective-permute-start(bf16[16,4096]{1,0:T(8,128)(2,1)S(1)} %get-tuple-element.42), channel_id=1, source_target_pairs={{0,1},{1,0},{2,3},{3,2},{4,5},{5,4},{6,7},{7,6},{8,9},{9,8},{10,11... | collective-permute-start | bytes 393224 | tf_op jit(solution)/shard_map/ppermute | solution.py:24
  85.9 11.9 %collective-permute-start.15 = (bf16[16,4096]{1,0:T(8,128)(2,1)S(1)}, bf16[16,4096]{1,0:T(8,128)(2,1)S(1)}, u32[]{:S(2)}, u32[]{:S(2)}) collective-permute-start(bf16[16,4096]{1,0:T(8,128)(2,1)S(1)} %get-tuple-element.43), channel_id=1, source_target_pairs={{0,2},{1,3},{2,0},{3,1},{4,6},{5,7},{6,4},{7,5},{8,10},{9,11},{10,... | collective-permute-start | bytes 393224 | tf_op jit(solution)/shard_map/ppermute | solution.py:24
  86.6 11.1 %collective-permute-start.16 = (bf16[16,4096]{1,0:T(8,128)(2,1)S(1)}, bf16[16,4096]{1,0:T(8,128)(2,1)S(1)}, u32[]{:S(2)}, u32[]{:S(2)}) collective-permute-start(bf16[16,4096]{1,0:T(8,128)(2,1)S(1)} %get-tuple-element.44), channel_id=1, source_target_pairs={{0,3},{1,2},{2,1},{3,0},{4,7},{5,6},{6,5},{7,4},{8,11},{9,10},{10,... | collective-permute-start | bytes 393224 | tf_op jit(solution)/shard_map/ppermute | solution.py:24
  97.8 15.6 %collective-permute-start.19 = (bf16[64,4096]{1,0:T(8,128)(2,1)S(1)}, bf16[64,4096]{1,0:T(8,128)(2,1)S(1)}, u32[]{:S(2)}, u32[]{:S(2)}) collective-permute-start(bf16[64,4096]{1,0:T(8,128)(2,1)S(1)} %get-tuple-element.60), channel_id=1, source_target_pairs={{0,8},{4,12},{8,0},{12,4},{16,24},{20,28},{24,16},{28,20},{1,9},{5... | collective-permute-start | bytes 1572872 | tf_op jit(solution)/shard_map/ppermute | solution.py:24
  99.7 13.3 %collective-permute-start.20 = (bf16[64,4096]{1,0:T(8,128)(2,1)S(1)}, bf16[64,4096]{1,0:T(8,128)(2,1)S(1)}, u32[]{:S(2)}, u32[]{:S(2)}) collective-permute-start(bf16[64,4096]{1,0:T(8,128)(2,1)S(1)} %get-tuple-element.60), channel_id=1, source_target_pairs={{0,16},{4,20},{8,24},{12,28},{16,0},{20,4},{24,8},{28,12},{1,17},{... | collective-permute-start | bytes 1572872 | tf_op jit(solution)/shard_map/ppermute | solution.py:24
  103.0 17.5 %collective-permute-start.23 = (bf16[64,4096]{1,0:T(8,128)(2,1)S(1)}, bf16[64,4096]{1,0:T(8,128)(2,1)S(1)}, u32[]{:S(2)}, u32[]{:S(2)}) collective-permute-start(bf16[64,4096]{1,0:T(8,128)(2,1)S(1)} %get-tuple-element.60), channel_id=1, source_target_pairs={{0,4},{4,0},{8,12},{12,8},{16,20},{20,16},{24,28},{28,24},{1,5},{5... | collective-permute-start | bytes 1572872 | tf_op jit(solution)/shard_map/ppermute | solution.py:24
  103.0 25.7 %collective-permute-start.17 = (bf16[2,64,2048]{2,1,0:T(8,128)(2,1)S(1)}, bf16[2,64,2048]{2,1,0:T(8,128)(2,1)S(1)}, u32[]{:S(2)}, u32[]{:S(2)}) collective-permute-start(bf16[2,64,2048]{2,1,0:T(8,128)(2,1)S(1)} %fusion.42), channel_id=1, source_target_pairs={{0,1},{1,0},{2,3},{3,2},{4,5},{5,4},{6,7},{7,6},{8,9},{9,8},{10,11... | collective-permute-start | bytes 1572872 | tf_op jit(solution)/shard_map/ppermute | solution.py:24
  106.3 26.2 %collective-permute-start.18 = (bf16[2,64,2048]{2,1,0:T(8,128)(2,1)S(1)}, bf16[2,64,2048]{2,1,0:T(8,128)(2,1)S(1)}, u32[]{:S(2)}, u32[]{:S(2)}) collective-permute-start(bf16[2,64,2048]{2,1,0:T(8,128)(2,1)S(1)} %fusion.57), channel_id=1, source_target_pairs={{0,2},{1,3},{2,0},{3,1},{4,6},{5,7},{6,4},{7,5},{8,10},{9,11},{10,... | collective-permute-start | bytes 1572872 | tf_op jit(solution)/shard_map/ppermute | solution.py:24
  113.0 6.8 %collective-permute-start.21 = (bf16[32,4096]{1,0:T(8,128)(2,1)S(1)}, bf16[32,4096]{1,0:T(8,128)(2,1)S(1)}, u32[]{:S(2)}, u32[]{:S(2)}) collective-permute-start(bf16[32,4096]{1,0:T(8,128)(2,1)S(1)} %slice.37), channel_id=1, source_target_pairs={{0,8},{4,12},{8,0},{12,4},{16,24},{20,28},{24,16},{28,20},{1,9},{5... | collective-permute-start | bytes 786440 | tf_op jit(solution)/shard_map/ppermute | solution.py:24
  113.5 6.8 %collective-permute-start.22 = (bf16[32,4096]{1,0:T(8,128)(2,1)S(1)}, bf16[32,4096]{1,0:T(8,128)(2,1)S(1)}, u32[]{:S(2)}, u32[]{:S(2)}) collective-permute-start(bf16[32,4096]{1,0:T(8,128)(2,1)S(1)} %slice.38), channel_id=1, source_target_pairs={{0,16},{4,20},{8,24},{12,28},{16,0},{20,4},{24,8},{28,12},{1,17},{... | collective-permute-start | bytes 786440 | tf_op jit(solution)/shard_map/ppermute | solution.py:24
  119.8 1.9 %collective-permute-start.24 = (bf16[64,4096]{1,0:T(8,128)(2,1)S(1)}, bf16[64,4096]{1,0:T(8,128)(2,1)S(1)}, u32[]{:S(2)}, u32[]{:S(2)}) collective-permute-start(bf16[64,4096]{1,0:T(8,128)(2,1)S(1)} %collective-permute-done.19), channel_id=1, source_target_pairs={{0,4},{4,0},{8,12},{12,8},{16,20},{20,16},{24,28},{28,24},{1,5},{5... | collective-permute-start | bytes 1572872 | tf_op jit(solution)/shard_map/ppermute | solution.py:24
  120.3 2.2 %collective-permute-start.25 = (bf16[64,4096]{1,0:T(8,128)(2,1)S(1)}, bf16[64,4096]{1,0:T(8,128)(2,1)S(1)}, u32[]{:S(2)}, u32[]{:S(2)}) collective-permute-start(bf16[64,4096]{1,0:T(8,128)(2,1)S(1)} %collective-permute-done.20), channel_id=1, source_target_pairs={{0,4},{4,0},{8,12},{12,8},{16,20},{20,16},{24,28},{28,24},{1,5},{5... | collective-permute-start | bytes 1572872 | tf_op jit(solution)/shard_map/ppermute | solution.py:24
  120.5 2.4 %collective-permute-start.26 = (bf16[32,4096]{1,0:T(8,128)(2,1)S(1)}, bf16[32,4096]{1,0:T(8,128)(2,1)S(1)}, u32[]{:S(2)}, u32[]{:S(2)}) collective-permute-start(bf16[32,4096]{1,0:T(8,128)(2,1)S(1)} %collective-permute-done.21), channel_id=1, source_target_pairs={{0,4},{4,0},{8,12},{12,8},{16,20},{20,16},{24,28},{28,24},{1,5},{5... | collective-permute-start | bytes 786440 | tf_op jit(solution)/shard_map/ppermute | solution.py:24
  121.7 1.5 %collective-permute-start.27 = (bf16[32,4096]{1,0:T(8,128)(2,1)S(1)}, bf16[32,4096]{1,0:T(8,128)(2,1)S(1)}, u32[]{:S(2)}, u32[]{:S(2)}) collective-permute-start(bf16[32,4096]{1,0:T(8,128)(2,1)S(1)} %collective-permute-done.22), channel_id=1, source_target_pairs={{0,4},{4,0},{8,12},{12,8},{16,20},{20,16},{24,28},{28,24},{1,5},{5... | collective-permute-start | bytes 786440 | tf_op jit(solution)/shard_map/ppermute | solution.py:24
  132.7 12.3 %collective-permute-start.29 = (bf16[64,2048]{1,0:T(8,128)(2,1)S(1)}, bf16[64,2048]{1,0:T(8,128)(2,1)S(1)}, u32[]{:S(2)}, u32[]{:S(2)}) collective-permute-start(bf16[64,2048]{1,0:T(8,128)(2,1)S(1)} %fusion.74), channel_id=1, source_target_pairs={{0,1},{1,0},{2,3},{3,2},{4,5},{5,4},{6,7},{7,6},{8,9},{9,8},{10,11... | collective-permute-start | bytes 786440 | tf_op jit(solution)/shard_map/ppermute | solution.py:24
  132.9 14.3 %copy-start.18 = (bf16[128,4096]{1,0:T(8,128)(2,1)S(1)}, bf16[128,4096]{1,0:T(8,128)(2,1)}, u32[]{:S(2)}) copy-start(bf16[128,4096]{1,0:T(8,128)(2,1)} %convolution_convert_fusion.1) | copy-start | bytes 3145732
  132.9 14.2 %collective-permute-start.28 = (bf16[64,2048]{1,0:T(8,128)(2,1)S(1)}, bf16[64,2048]{1,0:T(8,128)(2,1)S(1)}, u32[]{:S(2)}, u32[]{:S(2)}) collective-permute-start(bf16[64,2048]{1,0:T(8,128)(2,1)S(1)} %fusion.73), channel_id=1, source_target_pairs={{0,2},{1,3},{2,0},{3,1},{4,6},{5,7},{6,4},{7,5},{8,10},{9,11},{10,... | collective-permute-start | bytes 786440 | tf_op jit(solution)/shard_map/ppermute | solution.py:24

commit v3 on v2

--- a/solution.py
+++ b/solution.py
@@ -24,7 +24,7 @@
     return lax.ppermute(block, axis, [(i, i ^ distance) for i in range(count)])
 
 
-def gather_ctx(block, direct, rider=()):
+def gather_ctx(block, direct, rider=(), near=None):
     count = lax.axis_size("ctx")
     half = block.shape[0] // 2
     far = [(0, 0, block)]
@@ -39,11 +39,17 @@
         while distance < count:
             far += [(d ^ distance, first, swap(b, "ctx", distance)) for d, first, b in far]
             distance *= 2
+    if near is None:
+        late, _ = lax.optimization_barrier((block, far[1][2]))
+        near = swap(late, "ctx", 1)
     if rider:
         distance, first, last = far[-1]
         last, rider = lax.optimization_barrier((last, rider))
         far[-1] = (distance, first, last)
-    return far + [(d ^ 1, first, swap(b, "ctx", 1)) for d, first, b in far], rider
+    return far + [
+        (d ^ 1, first, near if b is block and near is not None else swap(b, "ctx", 1))
+        for d, first, b in far
+    ], rider
 
 
 def places_of(named):
@@ -257,12 +263,13 @@
     kv_head = column * heads_here // (QH // KVH)
     key_mine = lax.dynamic_slice_in_dim(keys, kv_head * HD, HD, 1)
     value_mine = lax.dynamic_slice_in_dim(values, kv_head * HD, HD, 1)
+    kv_pair = jnp.concatenate([key_mine, value_mine], axis=1)
+    kv_near = swap(kv_pair, "ctx", 1)
+    kv_near, routes = lax.optimization_barrier((kv_near, routes))
     routed = jnp.any(routes[:, :, None] == chosen[None, None, :], axis=1)
     named = jnp.any(routes[:, :, None] == chosen[None, None, :], axis=(1, 2)).astype(jnp.int32)
     named_all = [named[None]] + [swap(named[None], "exp", d) for d in range(1, exp_count)]
-    gathered, named_all = gather_ctx(
-        jnp.concatenate([key_mine, value_mine], axis=1), True, named_all
-    )
+    gathered, named_all = gather_ctx(kv_pair, True, named_all, near=kv_near)
     pieces = [piece for _, _, piece in gathered]
     blocks = [
         (distance, first // block_len + part)
@@ -279,9 +286,6 @@
     if first_rows < token_rows:
         chunks.append((first_rows, token_rows - first_rows))
     bits = exp_count.bit_length() - 1
-    residual_ordered = jnp.dot(order, residual, preferred_element_type=jnp.float32).astype(
-        jnp.bfloat16
-    )
     half = features // 2
     ways = (list(range(bits)), list(range(bits - 1, -1, -1)))
 
@@ -324,10 +328,14 @@
     sends = [project(attention, c, False) for c in range(2)]
     came = first_turn(sends)
     keeps = [project(attention, c, True) for c in range(2)]
+    _, residual = lax.optimization_barrier((sends, residual))
+    residual_ordered = jnp.dot(order, residual, preferred_element_type=jnp.float32).astype(
+        jnp.bfloat16
+    )
     if len(chunks) > 1:
         _, queries = lax.optimization_barrier((sends, queries))
         attention_late = attend_chunk(chunks[1], queries)
-        came, attention_late = lax.optimization_barrier((came, attention_late))
+        came, keeps, attention_late = lax.optimization_barrier((came, keeps, attention_late))
     keeps, came = other_turns(add_first(keeps, came))
 
     arrival = jnp.cumsum(routed.astype(jnp.int32), axis=0) - 1

time: 149 us -> 135 us (0.906); the launches traced: 149 us -> 136 us
  starting transfers between devices: 29 us -> 44.1 us
  Pallas kernels: 25.4 us -> 14.3 us
  matrix products: 21.9 us -> 14.3 us
  local copies, waits for them, and re-layouts: 9.77 us -> 3.77 us
  waiting for transfers between devices: 59.2 us -> 56.5 us
    ppermute x30, starting transfers between devices: 29 us -> 44.1 us  [swap(): return lax.ppermute(block, axis, [(i, i ^ distance) for i in range(count)])]
    pallas_call x2, Pallas kernels: 24.8 us -> 13.7 us  [attend(): pl.pallas_call(functools.partial(attend_kernel, start, tokens, block_len,...]
    dot_general x8, matrix products: 12.3 us -> 5.73 us  [project(): jnp.einsum('...rk,kd->...rd', picked, out_weight[:, columns * half:(colum...]
    unnamed x55 -> x21, local copies, waits for them, and re-layouts: 7.22 us -> 2.19 us
    ppermute x30, waiting for transfers between devices: 59.2 us -> 56.5 us  [swap(): return lax.ppermute(block, axis, [(i, i ^ distance) for i in range(count)])]
  transfers between devices with their start and end apart: 30 -> 30, of which waited for: 18 -> 21; matrix products, arithmetic and copies ran while one was open for 11% -> 11% of each run, Pallas kernels for 8% -> 5%
where the time goes in v3:
time: 135 us; the launch traced here: 136 us
  waiting for transfers between devices  56.5 us (42%)
  starting transfers between devices  44.1 us (33%)
  matrix products  14.3 us (11%)
  Pallas kernels  14.3 us (11%)
  local copies, waits for them, and re-layouts  3.77 us (3%)
  other arithmetic  2.37 us (2%)
    ppermute x30, waiting for transfers between devices, swap(): return lax.ppermute(block, axis, [(i, i ^ distance) for i in range(count)])  56.5 us
    ppermute x30, starting transfers between devices, swap(): return lax.ppermute(block, axis, [(i, i ^ distance) for i in range(count)])  44.1 us
    pallas_call x2, Pallas kernels, attend(): pl.pallas_call(functools.partial(attend_kernel, start, tokens, block_len,...  13.7 us
    dot_general x1, matrix products, local(): lax.dot_general(own_cols, every, (((0,), (0,)), ((), ())), preferred_elem...  5.79 us
    dot_general x8, matrix products, project(): jnp.einsum('...rk,kd->...rd', picked, out_weight[:, columns * half:(colum...  5.73 us
  transfers between devices with their start and end apart: 30, of which 21 were waited for; matrix products, arithmetic and copies ran while one was open for 11% of the time, Pallas kernels for 5%

profile of v3, /device:TPU:0, one launch (start us, length us, event | category | flops | bytes accessed | tf_op | source)
XLA Modules:
  0.0 136.5 jit_solution(6801714983753236934)
XLA Ops:
  0.7 1.1 constant_dynamic-slice_fusion.4
  1.8 0.5 collective-permute-start
  2.3 3.5 %collective-permute-start.1 = (bf16[512,256]{1,0:T(8,128)(2,1)S(1)}, bf16[512,256]{1,0:T(8,128)(2,1)S(1)}, u32[]{:S(2)}, u32[]{:S(2)}) collective-permute-start(bf16[512,256]{1,0:T(8,128)(2,1)S(1)} %pad_maximum_fusion.refs_4_), channel_id=1, source_target_pairs={{0,24},{4,28},{8,16},{12,20},{16,8},{20,12},{24,0},{28,4},{1,25},{... | collective-permute-start | bytes 786440 | tf_op jit(solution)/shard_map/ppermute | solution.py:24
  5.8 0.5 collective-permute-start.5
  6.5 0.8 compare_reduce_fusion
  7.3 2.0 %collective-permute-start.2 = (s32[1,128]{1,0:T(1,128)S(1)}, s32[1,128]{1,0:T(1,128)S(1)}, u32[]{:S(2)}, u32[]{:S(2)}) collective-permute-start(s32[1,128]{1,0:T(1,128)S(1)} %convert_bitcast_fusion.refs_0_), channel_id=1, source_target_pairs={{0,1},{1,0},{2,3},{3,2},{4,5},{5,4},{6,7},{7,6},{8,9},{9,8},{10,11... | collective-permute-start | bytes 1544 | tf_op jit(solution)/shard_map/ppermute | solution.py:24
  9.4 2.6 %collective-permute-start.3 = (s32[1,128]{1,0:T(1,128)S(1)}, s32[1,128]{1,0:T(1,128)S(1)}, u32[]{:S(2)}, u32[]{:S(2)}) collective-permute-start(s32[1,128]{1,0:T(1,128)S(1)} %convert_bitcast_fusion.refs_0_), channel_id=1, source_target_pairs={{0,2},{1,3},{2,0},{3,1},{4,6},{5,7},{6,4},{7,5},{8,10},{9,11},{10,... | collective-permute-start | bytes 1544 | tf_op jit(solution)/shard_map/ppermute | solution.py:24
  12.1 0.2 reduce_window_sum.11
  12.3 0.6 convert_reduce_fusion
  12.9 0.8 fusion.94
  13.6 3.4 %collective-permute-start.4 = (s32[1,128]{1,0:T(1,128)S(1)}, s32[1,128]{1,0:T(1,128)S(1)}, u32[]{:S(2)}, u32[]{:S(2)}) collective-permute-start(s32[1,128]{1,0:T(1,128)S(1)} %convert_bitcast_fusion.refs_0_), channel_id=1, source_target_pairs={{0,3},{1,2},{2,1},{3,0},{4,7},{5,6},{6,5},{7,4},{8,11},{9,10},{10,... | collective-permute-start | bytes 1544 | tf_op jit(solution)/shard_map/ppermute | solution.py:24
  17.1 1.5 %collective-permute-done.5.refs_5_ = bf16[512,256]{1,0:T(8,128)(2,1)S(1)} collective-permute-done((bf16[512,256]{1,0:T(8,128)(2,1)S(1)}, bf16[512,256]{1,0:T(8,128)(2,1)S(1)}, u32[]{:S(2)}, u32[]{:S(2)}) %collective-permute-start.5) | collective-permute-done | bytes 262176 | tf_op jit(solution)/shard_map/ppermute | solution.py:24
  18.7 0.5 collective-permute-start.8
  19.3 0.1 convolution_convert_fusion.2
  19.4 0.8 collective-permute-done.7.refs_9_
  20.2 0.4 collective-permute-done.8.refs_10_
  20.6 0.4 collective-permute-done.9.refs_11_
  20.9 1.2 copy-done.2
  22.2 0.7 copy-done.3
  22.8 6.8 %shard_map.104 = bf16[256,1024]{1,0:T(8,128)(2,1)S(1)} custom-call(s32[16]{0:T(128)S(1)} %copy-done.3, s32[2]{0:T(128)S(1)} %pad_add_fusion.rank_ref, bf16[512,1024]{1,0:T(8,128)(2,1)S(1)} %copy-done.2, s32[1,128]{1,0:T(1,128)S(1)} %convert_bitcast_fusion.refs_0_, s32[1,128]{1,0:T(1,128)S(1)} %collective-permute-done.2.refs_1_, ...), custom_call_target="tpu_custom_call" | custom-call | flops 4294967296 | bytes 6291456 | tf_op jit(solution)/shard_map/pallas_call | solution.py:181
  29.7 0.7 fusion.24
  30.4 1.6 %collective-permute-start.10 = (bf16[2,64,2048]{2,1,0:T(8,128)(2,1)S(1)}, bf16[2,64,2048]{2,1,0:T(8,128)(2,1)S(1)}, u32[]{:S(2)}, u32[]{:S(2)}) collective-permute-start(bf16[2,64,2048]{2,1,0:T(8,128)(2,1)S(1)} %fusion.24), channel_id=1, source_target_pairs={{0,1},{1,0},{2,3},{3,2},{4,5},{5,4},{6,7},{7,6},{8,9},{9,8},{10,11... | collective-permute-start | bytes 1572872 | tf_op jit(solution)/shard_map/ppermute | solution.py:24
  32.0 0.7 fusion.39
  32.8 2.7 %collective-permute-start.11 = (bf16[2,64,2048]{2,1,0:T(8,128)(2,1)S(1)}, bf16[2,64,2048]{2,1,0:T(8,128)(2,1)S(1)}, u32[]{:S(2)}, u32[]{:S(2)}) collective-permute-start(bf16[2,64,2048]{2,1,0:T(8,128)(2,1)S(1)} %fusion.39), channel_id=1, source_target_pairs={{0,2},{1,3},{2,0},{3,1},{4,6},{5,7},{6,4},{7,5},{8,10},{9,11},{10,... | collective-permute-start | bytes 1572872 | tf_op jit(solution)/shard_map/ppermute | solution.py:24
  35.4 0.7 fusion.27
  36.1 0.7 fusion.42
  36.9 0.4 convolution_convert_fusion.1
  37.4 6.9 %shard_map.105 = bf16[256,1024]{1,0:T(8,128)(2,1)S(1)} custom-call(s32[16]{0:T(128)S(1)} %copy-done.3, s32[2]{0:T(128)S(1)} %pad_add_fusion.rank_ref, bf16[512,1024]{1,0:T(8,128)(2,1)S(1)} %copy-done.2, s32[1,128]{1,0:T(1,128)S(1)} %convert_bitcast_fusion.refs_0_, s32[1,128]{1,0:T(1,128)S(1)} %collective-permute-done.2.refs_1_, ...), custom_call_target="tpu_custom_call" | custom-call | flops 4294967296 | bytes 6291456 | tf_op jit(solution)/shard_map/pallas_call | solution.py:181
  44.3 9.0 %collective-permute-done.10 = bf16[2,64,2048]{2,1,0:T(8,128)(2,1)S(1)} collective-permute-done((bf16[2,64,2048]{2,1,0:T(8,128)(2,1)S(1)}, bf16[2,64,2048]{2,1,0:T(8,128)(2,1)S(1)}, u32[]{:S(2)}, u32[]{:S(2)}) %collective-permute-start.10) | collective-permute-done | bytes 524320 | tf_op jit(solution)/shard_map/ppermute | solution.py:24
  53.2 0.3 collective-permute-done.11
  53.9 3.5 %collective-permute-start.12 = (bf16[64,2048]{1,0:T(8,128)(2,1)S(1)}, bf16[64,2048]{1,0:T(8,128)(2,1)S(1)}, u32[]{:S(2)}, u32[]{:S(2)}) collective-permute-start(bf16[64,2048]{1,0:T(8,128)(2,1)S(1)} %fusion.59), channel_id=1, source_target_pairs={{0,2},{1,3},{2,0},{3,1},{4,6},{5,7},{6,4},{7,5},{8,10},{9,11},{10,... | collective-permute-start | bytes 786440 | tf_op jit(solution)/shard_map/ppermute | solution.py:24
  57.4 4.2 %collective-permute-start.13 = (bf16[64,2048]{1,0:T(8,128)(2,1)S(1)}, bf16[64,2048]{1,0:T(8,128)(2,1)S(1)}, u32[]{:S(2)}, u32[]{:S(2)}) collective-permute-start(bf16[64,2048]{1,0:T(8,128)(2,1)S(1)} %fusion.60), channel_id=1, source_target_pairs={{0,1},{1,0},{2,3},{3,2},{4,5},{5,4},{6,7},{7,6},{8,9},{9,8},{10,11... | collective-permute-start | bytes 786440 | tf_op jit(solution)/shard_map/ppermute | solution.py:24
  61.7 5.8 %collective-permute-done.12.refs_2_ = bf16[64,2048]{1,0:T(8,128)(2,1)S(1)} collective-permute-done((bf16[64,2048]{1,0:T(8,128)(2,1)S(1)}, bf16[64,2048]{1,0:T(8,128)(2,1)S(1)}, u32[]{:S(2)}, u32[]{:S(2)}) %collective-permute-start.12) | collective-permute-done | bytes 262176 | tf_op jit(solution)/shard_map/ppermute | solution.py:24
  67.5 1.2 collective-permute-done.13.refs_3_
  68.8 0.6 shard_map.106
  69.3 2.3 %collective-permute-start.14 = (bf16[16,4096]{1,0:T(8,128)(2,1)S(1)}, bf16[16,4096]{1,0:T(8,128)(2,1)S(1)}, u32[]{:S(2)}, u32[]{:S(2)}) collective-permute-start(bf16[16,4096]{1,0:T(8,128)(2,1)S(1)} %get-tuple-element.53), channel_id=1, source_target_pairs={{0,1},{1,0},{2,3},{3,2},{4,5},{5,4},{6,7},{7,6},{8,9},{9,8},{10,11... | collective-permute-start | bytes 393224 | tf_op jit(solution)/shard_map/ppermute | solution.py:24
  71.6 4.0 %collective-permute-start.15 = (bf16[16,4096]{1,0:T(8,128)(2,1)S(1)}, bf16[16,4096]{1,0:T(8,128)(2,1)S(1)}, u32[]{:S(2)}, u32[]{:S(2)}) collective-permute-start(bf16[16,4096]{1,0:T(8,128)(2,1)S(1)} %get-tuple-element.54), channel_id=1, source_target_pairs={{0,2},{1,3},{2,0},{3,1},{4,6},{5,7},{6,4},{7,5},{8,10},{9,11},{10,... | collective-permute-start | bytes 393224 | tf_op jit(solution)/shard_map/ppermute | solution.py:24
  75.7 0.7 fusion.36
  76.4 0.7 fusion.45
  77.1 2.6 %collective-permute-done.15 = bf16[16,4096]{1,0:T(8,128)(2,1)S(1)} collective-permute-done((bf16[16,4096]{1,0:T(8,128)(2,1)S(1)}, bf16[16,4096]{1,0:T(8,128)(2,1)S(1)}, u32[]{:S(2)}, u32[]{:S(2)}) %collective-permute-start.15) | collective-permute-done | bytes 131104 | tf_op jit(solution)/shard_map/ppermute | solution.py:24
  79.8 5.8 %collective-permute-done.16 = bf16[16,4096]{1,0:T(8,128)(2,1)S(1)} collective-permute-done((bf16[16,4096]{1,0:T(8,128)(2,1)S(1)}, bf16[16,4096]{1,0:T(8,128)(2,1)S(1)}, u32[]{:S(2)}, u32[]{:S(2)}) %collective-permute-start.16) | collective-permute-done | bytes 131104 | tf_op jit(solution)/shard_map/ppermute | solution.py:24
  85.7 8.8 %collective-permute-start.19 = (bf16[64,4096]{1,0:T(8,128)(2,1)S(1)}, bf16[64,4096]{1,0:T(8,128)(2,1)S(1)}, u32[]{:S(2)}, u32[]{:S(2)}) collective-permute-start(bf16[64,4096]{1,0:T(8,128)(2,1)S(1)} %get-tuple-element.64), channel_id=1, source_target_pairs={{0,8},{4,12},{8,0},{12,4},{16,24},{20,28},{24,16},{28,20},{1,9},{5... | collective-permute-start | bytes 1572872 | tf_op jit(solution)/shard_map/ppermute | solution.py:24
  94.4 0.7 fusion.33
  95.2 0.7 fusion.51
  95.9 2.3 %collective-permute-start.17 = (bf16[2,64,2048]{2,1,0:T(8,128)(2,1)S(1)}, bf16[2,64,2048]{2,1,0:T(8,128)(2,1)S(1)}, u32[]{:S(2)}, u32[]{:S(2)}) collective-permute-start(bf16[2,64,2048]{2,1,0:T(8,128)(2,1)S(1)} %fusion.36), channel_id=1, source_target_pairs={{0,1},{1,0},{2,3},{3,2},{4,5},{5,4},{6,7},{7,6},{8,9},{9,8},{10,11... | collective-permute-start | bytes 1572872 | tf_op jit(solution)/shard_map/ppermute | solution.py:24
  98.2 7.8 %collective-permute-done.20 = bf16[64,4096]{1,0:T(8,128)(2,1)S(1)} collective-permute-done((bf16[64,4096]{1,0:T(8,128)(2,1)S(1)}, bf16[64,4096]{1,0:T(8,128)(2,1)S(1)}, u32[]{:S(2)}, u32[]{:S(2)}) %collective-permute-start.20) | collective-permute-done | bytes 524320 | tf_op jit(solution)/shard_map/ppermute | solution.py:24
  106.0 0.2 collective-permute-start.21
  106.2 0.4 collective-permute-start.22
  106.7 5.8 %collective-permute-done.21 = bf16[32,4096]{1,0:T(8,128)(2,1)S(1)} collective-permute-done((bf16[32,4096]{1,0:T(8,128)(2,1)S(1)}, bf16[32,4096]{1,0:T(8,128)(2,1)S(1)}, u32[]{:S(2)}, u32[]{:S(2)}) %collective-permute-start.21) | collective-permute-done | bytes 262176 | tf_op jit(solution)/shard_map/ppermute | solution.py:24
  112.5 0.2 collective-permute-done.22
  112.7 0.4 collective-permute-start.25
  113.1 0.2 collective-permute-start.26
  113.3 1.0 collective-permute-done.24
  114.4 0.1 collective-permute-start.27
  114.5 0.6 collective-permute-done.25
  115.2 0.3 collective-permute-done.26
  115.5 0.4 collective-permute-done.27
  115.9 2.4 %collective-permute-done.17 = bf16[2,64,2048]{2,1,0:T(8,128)(2,1)S(1)} collective-permute-done((bf16[2,64,2048]{2,1,0:T(8,128)(2,1)S(1)}, bf16[2,64,2048]{2,1,0:T(8,128)(2,1)S(1)}, u32[]{:S(2)}, u32[]{:S(2)}) %collective-permute-start.17) | collective-permute-done | bytes 524320 | tf_op jit(solution)/shard_map/ppermute | solution.py:24
  118.3 4.4 %collective-permute-done.18 = bf16[2,64,2048]{2,1,0:T(8,128)(2,1)S(1)} collective-permute-done((bf16[2,64,2048]{2,1,0:T(8,128)(2,1)S(1)}, bf16[2,64,2048]{2,1,0:T(8,128)(2,1)S(1)}, u32[]{:S(2)}, u32[]{:S(2)}) %collective-permute-start.18) | collective-permute-done | bytes 524320 | tf_op jit(solution)/shard_map/ppermute | solution.py:24
  123.1 0.2 collective-permute-start.28
  123.3 5.8 %multiply_bitcast_fusion = f32[1,512,4096]{2,1,0:T(8,128)} fusion(bf16[512,4096]{1,0:T(8,128)(2,1)S(1)} %constant_dynamic-update-slice_fusion.4, s32[]{:T(128)S(6)} %select_n.73), kind=kOutput, calls=%fused_computation | convolution fusion | flops 2149580800 | bytes 13107204 | tf_op jit(solution)/shard_map/dot_general | solution.py:381
  129.1 3.9 %collective-permute-done.29 = bf16[64,2048]{1,0:T(8,128)(2,1)S(1)} collective-permute-done((bf16[64,2048]{1,0:T(8,128)(2,1)S(1)}, bf16[64,2048]{1,0:T(8,128)(2,1)S(1)}, u32[]{:S(2)}, u32[]{:S(2)}) %collective-permute-start.29) | collective-permute-done | bytes 262176 | tf_op jit(solution)/shard_map/ppermute | solution.py:24
  133.0 1.9 %collective-permute-done.28 = bf16[64,2048]{1,0:T(8,128)(2,1)S(1)} collective-permute-done((bf16[64,2048]{1,0:T(8,128)(2,1)S(1)}, bf16[64,2048]{1,0:T(8,128)(2,1)S(1)}, u32[]{:S(2)}, u32[]{:S(2)}) %collective-permute-start.28) | collective-permute-done | bytes 262176 | tf_op jit(solution)/shard_map/ppermute | solution.py:24
  135.0 1.5 %convolution_convert_fusion = bf16[128,4096]{1,0:T(8,128)(2,1)} fusion(bf16[64,4096]{1,0:T(8,128)(2,1)S(1)} %fusion.54, bf16[64,4096]{1,0:T(8,128)(2,1)S(1)} %get-tuple-element.51, s32[128]{0:T(128)S(1)} %fusion.94), kind=kOutput, calls=%fused_computation.1 | convolution fusion | flops 136855552 | bytes 2097664 | tf_op jit(solution)/shard_map/dot_general | solution.py:376
  (65 shorter events, 1.9 us)
Async XLA Ops:
  0.6 36.2 %copy-start = (bf16[128,4096]{1,0:T(8,128)(2,1)S(1)}, bf16[128,4096]{1,0:T(8,128)(2,1)}, u32[]{:S(2)}) copy-start(bf16[128,4096]{1,0:T(8,128)(2,1)} %param.12) | copy-start | bytes 3145732
  1.8 4.8 %collective-permute-start = (bf16[512,256]{1,0:T(8,128)(2,1)S(1)}, bf16[512,256]{1,0:T(8,128)(2,1)S(1)}, u32[]{:S(2)}, u32[]{:S(2)}) collective-permute-start(bf16[512,256]{1,0:T(8,128)(2,1)S(1)} %pad_maximum_fusion.refs_4_), channel_id=1, source_target_pairs={{0,4},{4,0},{8,12},{12,8},{16,20},{20,16},{24,28},{28,24},{1,5},{5... | collective-permute-start | bytes 786440 | tf_op jit(solution)/shard_map/ppermute | solution.py:24
  2.3 11.3 %collective-permute-start.1 = (bf16[512,256]{1,0:T(8,128)(2,1)S(1)}, bf16[512,256]{1,0:T(8,128)(2,1)S(1)}, u32[]{:S(2)}, u32[]{:S(2)}) collective-permute-start(bf16[512,256]{1,0:T(8,128)(2,1)S(1)} %pad_maximum_fusion.refs_4_), channel_id=1, source_target_pairs={{0,24},{4,28},{8,16},{12,20},{16,8},{20,12},{24,0},{28,4},{1,25},{... | collective-permute-start | bytes 786440 | tf_op jit(solution)/shard_map/ppermute | solution.py:24
  5.8 12.8 %collective-permute-start.5 = (bf16[512,256]{1,0:T(8,128)(2,1)S(1)}, bf16[512,256]{1,0:T(8,128)(2,1)S(1)}, u32[]{:S(2)}, u32[]{:S(2)}) collective-permute-start(bf16[512,256]{1,0:T(8,128)(2,1)S(1)} %pad_maximum_fusion.refs_4_), channel_id=1, source_target_pairs={{0,8},{4,12},{8,0},{12,4},{16,24},{20,28},{24,16},{28,20},{1,9},{5... | collective-permute-start | bytes 786440 | tf_op jit(solution)/shard_map/ppermute | solution.py:24
  6.4 12.3 %collective-permute-start.6 = (bf16[512,256]{1,0:T(8,128)(2,1)S(1)}, bf16[512,256]{1,0:T(8,128)(2,1)S(1)}, u32[]{:S(2)}, u32[]{:S(2)}) collective-permute-start(bf16[512,256]{1,0:T(8,128)(2,1)S(1)} %pad_maximum_fusion.refs_4_), channel_id=1, source_target_pairs={{0,16},{4,20},{8,24},{12,28},{16,0},{20,4},{24,8},{28,12},{1,17},{... | collective-permute-start | bytes 786440 | tf_op jit(solution)/shard_map/ppermute | solution.py:24
  7.3 11.8 %collective-permute-start.2 = (s32[1,128]{1,0:T(1,128)S(1)}, s32[1,128]{1,0:T(1,128)S(1)}, u32[]{:S(2)}, u32[]{:S(2)}) collective-permute-start(s32[1,128]{1,0:T(1,128)S(1)} %convert_bitcast_fusion.refs_0_), channel_id=1, source_target_pairs={{0,1},{1,0},{2,3},{3,2},{4,5},{5,4},{6,7},{7,6},{8,9},{9,8},{10,11... | collective-permute-start | bytes 1544 | tf_op jit(solution)/shard_map/ppermute | solution.py:24
  9.4 9.8 %collective-permute-start.3 = (s32[1,128]{1,0:T(1,128)S(1)}, s32[1,128]{1,0:T(1,128)S(1)}, u32[]{:S(2)}, u32[]{:S(2)}) collective-permute-start(s32[1,128]{1,0:T(1,128)S(1)} %convert_bitcast_fusion.refs_0_), channel_id=1, source_target_pairs={{0,2},{1,3},{2,0},{3,1},{4,6},{5,7},{6,4},{7,5},{8,10},{9,11},{10,... | collective-permute-start | bytes 1544 | tf_op jit(solution)/shard_map/ppermute | solution.py:24
  13.6 5.5 %collective-permute-start.4 = (s32[1,128]{1,0:T(1,128)S(1)}, s32[1,128]{1,0:T(1,128)S(1)}, u32[]{:S(2)}, u32[]{:S(2)}) collective-permute-start(s32[1,128]{1,0:T(1,128)S(1)} %convert_bitcast_fusion.refs_0_), channel_id=1, source_target_pairs={{0,3},{1,2},{2,1},{3,0},{4,7},{5,6},{6,5},{7,4},{8,11},{9,10},{10,... | collective-permute-start | bytes 1544 | tf_op jit(solution)/shard_map/ppermute | solution.py:24
  18.6 1.5 %collective-permute-start.7 = (bf16[512,256]{1,0:T(8,128)(2,1)S(1)}, bf16[512,256]{1,0:T(8,128)(2,1)S(1)}, u32[]{:S(2)}, u32[]{:S(2)}) collective-permute-start(bf16[512,256]{1,0:T(8,128)(2,1)S(1)} %collective-permute-done.5.refs_5_), channel_id=1, source_target_pairs={{0,4},{4,0},{8,12},{12,8},{16,20},{20,16},{24,28},{28,24},{1,5},{5... | collective-permute-start | bytes 786440 | tf_op jit(solution)/shard_map/ppermute | solution.py:24
  18.7 1.9 %collective-permute-start.8 = (bf16[512,256]{1,0:T(8,128)(2,1)S(1)}, bf16[512,256]{1,0:T(8,128)(2,1)S(1)}, u32[]{:S(2)}, u32[]{:S(2)}) collective-permute-start(bf16[512,256]{1,0:T(8,128)(2,1)S(1)} %collective-permute-done.6.refs_6_), channel_id=1, source_target_pairs={{0,4},{4,0},{8,12},{12,8},{16,20},{20,16},{24,28},{28,24},{1,5},{5... | collective-permute-start | bytes 786440 | tf_op jit(solution)/shard_map/ppermute | solution.py:24
  19.2 1.8 %collective-permute-start.9 = (bf16[512,256]{1,0:T(8,128)(2,1)S(1)}, bf16[512,256]{1,0:T(8,128)(2,1)S(1)}, u32[]{:S(2)}, u32[]{:S(2)}) collective-permute-start(bf16[512,256]{1,0:T(8,128)(2,1)S(1)} %collective-permute-done.1.refs_7_), channel_id=1, source_target_pairs={{0,4},{4,0},{8,12},{12,8},{16,20},{20,16},{24,28},{28,24},{1,5},{5... | collective-permute-start | bytes 786440 | tf_op jit(solution)/shard_map/ppermute | solution.py:24
  20.9 1.2 copy-start.2
  22.2 0.7 copy-start.3
  22.8 6.8 %copy-start.4 = (bf16[1024,4096]{1,0:T(8,128)(2,1)S(1)}, bf16[1024,4096]{1,0:T(8,128)(2,1)}, u32[]{:S(2)}) copy-start(bf16[1024,4096]{1,0:T(8,128)(2,1)} %param.13) | copy-start | bytes 25165828
  30.4 22.8 %collective-permute-start.10 = (bf16[2,64,2048]{2,1,0:T(8,128)(2,1)S(1)}, bf16[2,64,2048]{2,1,0:T(8,128)(2,1)S(1)}, u32[]{:S(2)}, u32[]{:S(2)}) collective-permute-start(bf16[2,64,2048]{2,1,0:T(8,128)(2,1)S(1)} %fusion.24), channel_id=1, source_target_pairs={{0,1},{1,0},{2,3},{3,2},{4,5},{5,4},{6,7},{7,6},{8,9},{9,8},{10,11... | collective-permute-start | bytes 1572872 | tf_op jit(solution)/shard_map/ppermute | solution.py:24
  32.8 20.8 %collective-permute-start.11 = (bf16[2,64,2048]{2,1,0:T(8,128)(2,1)S(1)}, bf16[2,64,2048]{2,1,0:T(8,128)(2,1)S(1)}, u32[]{:S(2)}, u32[]{:S(2)}) collective-permute-start(bf16[2,64,2048]{2,1,0:T(8,128)(2,1)S(1)} %fusion.39), channel_id=1, source_target_pairs={{0,2},{1,3},{2,0},{3,1},{4,6},{5,7},{6,4},{7,5},{8,10},{9,11},{10,... | collective-permute-start | bytes 1572872 | tf_op jit(solution)/shard_map/ppermute | solution.py:24
  44.3 24.5 %copy-start.1 = (f32[4096]{0:T(1024)S(1)}, f32[4096]{0:T(1024)}, u32[]{:S(2)}) copy-start(f32[4096]{0:T(1024)} %param.14) | copy-start | bytes 49156
  53.9 13.6 %collective-permute-start.12 = (bf16[64,2048]{1,0:T(8,128)(2,1)S(1)}, bf16[64,2048]{1,0:T(8,128)(2,1)S(1)}, u32[]{:S(2)}, u32[]{:S(2)}) collective-permute-start(bf16[64,2048]{1,0:T(8,128)(2,1)S(1)} %fusion.59), channel_id=1, source_target_pairs={{0,2},{1,3},{2,0},{3,1},{4,6},{5,7},{6,4},{7,5},{8,10},{9,11},{10,... | collective-permute-start | bytes 786440 | tf_op jit(solution)/shard_map/ppermute | solution.py:24
  57.4 11.3 %collective-permute-start.13 = (bf16[64,2048]{1,0:T(8,128)(2,1)S(1)}, bf16[64,2048]{1,0:T(8,128)(2,1)S(1)}, u32[]{:S(2)}, u32[]{:S(2)}) collective-permute-start(bf16[64,2048]{1,0:T(8,128)(2,1)S(1)} %fusion.60), channel_id=1, source_target_pairs={{0,1},{1,0},{2,3},{3,2},{4,5},{5,4},{6,7},{7,6},{8,9},{9,8},{10,11... | collective-permute-start | bytes 786440 | tf_op jit(solution)/shard_map/ppermute | solution.py:24
  69.3 7.8 %collective-permute-start.14 = (bf16[16,4096]{1,0:T(8,128)(2,1)S(1)}, bf16[16,4096]{1,0:T(8,128)(2,1)S(1)}, u32[]{:S(2)}, u32[]{:S(2)}) collective-permute-start(bf16[16,4096]{1,0:T(8,128)(2,1)S(1)} %get-tuple-element.53), channel_id=1, source_target_pairs={{0,1},{1,0},{2,3},{3,2},{4,5},{5,4},{6,7},{7,6},{8,9},{9,8},{10,11... | collective-permute-start | bytes 393224 | tf_op jit(solution)/shard_map/ppermute | solution.py:24
  71.6 8.1 %collective-permute-start.15 = (bf16[16,4096]{1,0:T(8,128)(2,1)S(1)}, bf16[16,4096]{1,0:T(8,128)(2,1)S(1)}, u32[]{:S(2)}, u32[]{:S(2)}) collective-permute-start(bf16[16,4096]{1,0:T(8,128)(2,1)S(1)} %get-tuple-element.54), channel_id=1, source_target_pairs={{0,2},{1,3},{2,0},{3,1},{4,6},{5,7},{6,4},{7,5},{8,10},{9,11},{10,... | collective-permute-start | bytes 393224 | tf_op jit(solution)/shard_map/ppermute | solution.py:24
  75.7 9.9 %collective-permute-start.16 = (bf16[16,4096]{1,0:T(8,128)(2,1)S(1)}, bf16[16,4096]{1,0:T(8,128)(2,1)S(1)}, u32[]{:S(2)}, u32[]{:S(2)}) collective-permute-start(bf16[16,4096]{1,0:T(8,128)(2,1)S(1)} %get-tuple-element.55), channel_id=1, source_target_pairs={{0,3},{1,2},{2,1},{3,0},{4,7},{5,6},{6,5},{7,4},{8,11},{9,10},{10,... | collective-permute-start | bytes 393224 | tf_op jit(solution)/shard_map/ppermute | solution.py:24
  85.7 20.5 %collective-permute-start.19 = (bf16[64,4096]{1,0:T(8,128)(2,1)S(1)}, bf16[64,4096]{1,0:T(8,128)(2,1)S(1)}, u32[]{:S(2)}, u32[]{:S(2)}) collective-permute-start(bf16[64,4096]{1,0:T(8,128)(2,1)S(1)} %get-tuple-element.64), channel_id=1, source_target_pairs={{0,8},{4,12},{8,0},{12,4},{16,24},{20,28},{24,16},{28,20},{1,9},{5... | collective-permute-start | bytes 1572872 | tf_op jit(solution)/shard_map/ppermute | solution.py:24
  94.4 11.6 %collective-permute-start.20 = (bf16[64,4096]{1,0:T(8,128)(2,1)S(1)}, bf16[64,4096]{1,0:T(8,128)(2,1)S(1)}, u32[]{:S(2)}, u32[]{:S(2)}) collective-permute-start(bf16[64,4096]{1,0:T(8,128)(2,1)S(1)} %get-tuple-element.64), channel_id=1, source_target_pairs={{0,16},{4,20},{8,24},{12,28},{16,0},{20,4},{24,8},{28,12},{1,17},{... | collective-permute-start | bytes 1572872 | tf_op jit(solution)/shard_map/ppermute | solution.py:24
  95.9 22.4 %collective-permute-start.17 = (bf16[2,64,2048]{2,1,0:T(8,128)(2,1)S(1)}, bf16[2,64,2048]{2,1,0:T(8,128)(2,1)S(1)}, u32[]{:S(2)}, u32[]{:S(2)}) collective-permute-start(bf16[2,64,2048]{2,1,0:T(8,128)(2,1)S(1)} %fusion.36), channel_id=1, source_target_pairs={{0,1},{1,0},{2,3},{3,2},{4,5},{5,4},{6,7},{7,6},{8,9},{9,8},{10,11... | collective-permute-start | bytes 1572872 | tf_op jit(solution)/shard_map/ppermute | solution.py:24
  98.1 24.5 %collective-permute-start.18 = (bf16[2,64,2048]{2,1,0:T(8,128)(2,1)S(1)}, bf16[2,64,2048]{2,1,0:T(8,128)(2,1)S(1)}, u32[]{:S(2)}, u32[]{:S(2)}) collective-permute-start(bf16[2,64,2048]{2,1,0:T(8,128)(2,1)S(1)} %fusion.45), channel_id=1, source_target_pairs={{0,2},{1,3},{2,0},{3,1},{4,6},{5,7},{6,4},{7,5},{8,10},{9,11},{10,... | collective-permute-start | bytes 1572872 | tf_op jit(solution)/shard_map/ppermute | solution.py:24
  106.0 6.4 %collective-permute-start.21 = (bf16[32,4096]{1,0:T(8,128)(2,1)S(1)}, bf16[32,4096]{1,0:T(8,128)(2,1)S(1)}, u32[]{:S(2)}, u32[]{:S(2)}) collective-permute-start(bf16[32,4096]{1,0:T(8,128)(2,1)S(1)} %slice.37), channel_id=1, source_target_pairs={{0,8},{4,12},{8,0},{12,4},{16,24},{20,28},{24,16},{28,20},{1,9},{5... | collective-permute-start | bytes 786440 | tf_op jit(solution)/shard_map/ppermute | solution.py:24
  106.2 6.4 %collective-permute-start.22 = (bf16[32,4096]{1,0:T(8,128)(2,1)S(1)}, bf16[32,4096]{1,0:T(8,128)(2,1)S(1)}, u32[]{:S(2)}, u32[]{:S(2)}) collective-permute-start(bf16[32,4096]{1,0:T(8,128)(2,1)S(1)} %slice.38), channel_id=1, source_target_pairs={{0,16},{4,20},{8,24},{12,28},{16,0},{20,4},{24,8},{28,12},{1,17},{... | collective-permute-start | bytes 786440 | tf_op jit(solution)/shard_map/ppermute | solution.py:24
  106.6 6.5 %collective-permute-start.23 = (bf16[64,4096]{1,0:T(8,128)(2,1)S(1)}, bf16[64,4096]{1,0:T(8,128)(2,1)S(1)}, u32[]{:S(2)}, u32[]{:S(2)}) collective-permute-start(bf16[64,4096]{1,0:T(8,128)(2,1)S(1)} %get-tuple-element.64), channel_id=1, source_target_pairs={{0,4},{4,0},{8,12},{12,8},{16,20},{20,16},{24,28},{28,24},{1,5},{5... | collective-permute-start | bytes 1572872 | tf_op jit(solution)/shard_map/ppermute | solution.py:24
  112.5 1.9 %collective-permute-start.24 = (bf16[64,4096]{1,0:T(8,128)(2,1)S(1)}, bf16[64,4096]{1,0:T(8,128)(2,1)S(1)}, u32[]{:S(2)}, u32[]{:S(2)}) collective-permute-start(bf16[64,4096]{1,0:T(8,128)(2,1)S(1)} %collective-permute-done.19), channel_id=1, source_target_pairs={{0,4},{4,0},{8,12},{12,8},{16,20},{20,16},{24,28},{28,24},{1,5},{5... | collective-permute-start | bytes 1572872 | tf_op jit(solution)/shard_map/ppermute | solution.py:24
  112.7 2.4 %collective-permute-start.25 = (bf16[64,4096]{1,0:T(8,128)(2,1)S(1)}, bf16[64,4096]{1,0:T(8,128)(2,1)S(1)}, u32[]{:S(2)}, u32[]{:S(2)}) collective-permute-start(bf16[64,4096]{1,0:T(8,128)(2,1)S(1)} %collective-permute-done.20), channel_id=1, source_target_pairs={{0,4},{4,0},{8,12},{12,8},{16,20},{20,16},{24,28},{28,24},{1,5},{5... | collective-permute-start | bytes 1572872 | tf_op jit(solution)/shard_map/ppermute | solution.py:24
  113.1 2.4 %collective-permute-start.26 = (bf16[32,4096]{1,0:T(8,128)(2,1)S(1)}, bf16[32,4096]{1,0:T(8,128)(2,1)S(1)}, u32[]{:S(2)}, u32[]{:S(2)}) collective-permute-start(bf16[32,4096]{1,0:T(8,128)(2,1)S(1)} %collective-permute-done.21), channel_id=1, source_target_pairs={{0,4},{4,0},{8,12},{12,8},{16,20},{20,16},{24,28},{28,24},{1,5},{5... | collective-permute-start | bytes 786440 | tf_op jit(solution)/shard_map/ppermute | solution.py:24
  114.4 1.5 %collective-permute-start.27 = (bf16[32,4096]{1,0:T(8,128)(2,1)S(1)}, bf16[32,4096]{1,0:T(8,128)(2,1)S(1)}, u32[]{:S(2)}, u32[]{:S(2)}) collective-permute-start(bf16[32,4096]{1,0:T(8,128)(2,1)S(1)} %collective-permute-done.22), channel_id=1, source_target_pairs={{0,4},{4,0},{8,12},{12,8},{16,20},{20,16},{24,28},{28,24},{1,5},{5... | collective-permute-start | bytes 786440 | tf_op jit(solution)/shard_map/ppermute | solution.py:24
  122.9 10.0 %collective-permute-start.29 = (bf16[64,2048]{1,0:T(8,128)(2,1)S(1)}, bf16[64,2048]{1,0:T(8,128)(2,1)S(1)}, u32[]{:S(2)}, u32[]{:S(2)}) collective-permute-start(bf16[64,2048]{1,0:T(8,128)(2,1)S(1)} %fusion.62), channel_id=1, source_target_pairs={{0,1},{1,0},{2,3},{3,2},{4,5},{5,4},{6,7},{7,6},{8,9},{9,8},{10,11... | collective-permute-start | bytes 786440 | tf_op jit(solution)/shard_map/ppermute | solution.py:24
  123.1 11.8 %collective-permute-start.28 = (bf16[64,2048]{1,0:T(8,128)(2,1)S(1)}, bf16[64,2048]{1,0:T(8,128)(2,1)S(1)}, u32[]{:S(2)}, u32[]{:S(2)}) collective-permute-start(bf16[64,2048]{1,0:T(8,128)(2,1)S(1)} %fusion.61), channel_id=1, source_target_pairs={{0,2},{1,3},{2,0},{3,1},{4,6},{5,7},{6,4},{7,5},{8,10},{9,11},{10,... | collective-permute-start | bytes 786440 | tf_op jit(solution)/shard_map/ppermute | solution.py:24
